TPU v7x, 32 devices: a whole 2x2x4 slice. The times are simulated.
32 devices in a mesh: grid: 8 (over y, x, core), pair: 4 (over z).
Axes of the slice: x: 2, y: 2, z: 4, core: 2. Of those that a mesh axis runs over, the one named last changes fastest.
Arguments:
- orbitals: bfloat16 [64, 16, 4096], P('grid', None, 'pair'), may hold values from -6 to 6
- box_list: int32 [8, 4, 4], replicated, may hold values from 0 to 15, all different within a row
- pair_slots: int32 [8, 4, 4, 2], P('grid', 'pair'), may hold values from 0 to 3, as said below
- offsets: int32 [8, 4, 4, 3], P('grid', 'pair'), may hold values from -8 to 8
- pair_count: int32 [8, 4], P('grid', 'pair'), may hold values from 2 to 4, as said below
Outputs:
- exchange_field: float32 [64, 16, 4096], P('grid', None, 'pair')
Inputs may be any that keep to these rules, and one draw needn't show every extreme that they name: `box_list`: the 4 orbitals of one worker's list are all different. `pair_slots`: only the first pair_count entries of a worker's lists are used; the first 2 pairs of every worker name each slot of its list exactly once. `pair_count`: each group of 4 workers that share a grid index holds 12 pairs, and one of them holds 4.
All inputs are finite; a program needn't handle non-finite values.
Results may differ from a plain program's by a relative error of at most 0.0019.
Values may be sent and summed in bfloat16 or wider, within the bound.
No kernel may reach another device: no remote copies, remote signals or barrier semaphores. Data moves between devices by JAX's collectives and lax.ppermute only.
A program may use at most 128 MiB of HBM per device.

v0:
```python
import math

import jax
import jax.numpy as jnp
from jax import lax
from jax.sharding import PartitionSpec as P

SHIFT = 8


screening = 0.02


def cas_table(extent):
    places = jnp.arange(extent, dtype=jnp.int32)
    product = places[:, None] * places[None, :] % extent
    phases = product.astype(jnp.float32) * (2.0 * math.pi / extent)
    return jnp.cos(phases) + jnp.sin(phases)


def green_table(extent):
    phases = jnp.arange(extent, dtype=jnp.int32).astype(jnp.float32) * (2.0 * math.pi / extent)
    eigen = 2.0 - 2.0 * jnp.cos(phases)
    denominator = screening + eigen[:, None, None] + eigen[None, :, None] + eigen[None, None, :]
    return 1.0 / (denominator * float(extent**3))


def poisson(density, table, green):
    high = lax.Precision.HIGHEST
    spectrum = jnp.einsum("ax,xyz->ayz", table, density, precision=high)
    spectrum = jnp.einsum("by,ayz->abz", table, spectrum, precision=high)
    spectrum = jnp.einsum("cz,abz->abc", table, spectrum, precision=high)
    spectrum = spectrum * green
    spectrum = jnp.einsum("ax,xyz->ayz", table, spectrum, precision=high)
    spectrum = jnp.einsum("by,ayz->abz", table, spectrum, precision=high)
    return jnp.einsum("cz,abz->abc", table, spectrum, precision=high)


def shift_box(field, step_x, step_y, step_z):
    extent = field.shape[0]
    padded = jnp.pad(field, SHIFT)
    starts = (SHIFT + step_x, SHIFT + step_y, SHIFT + step_z)
    return lax.dynamic_slice(padded, starts, (extent, extent, extent))


def worker_fields(box_data, slot_list, offset_list, pair_total):
    extent = box_data.shape[0]
    capacity = box_data.shape[1]
    table = cas_table(extent)
    green = green_table(extent)

    def fetch(slot):
        picked = lax.dynamic_index_in_dim(box_data, slot, 1, False)
        return picked.astype(jnp.float32).reshape(extent, extent, extent)

    def add_slot(collected, slot, value):
        current = lax.dynamic_index_in_dim(collected, slot, 1, True)
        updated = current + value.reshape(extent, 1, extent * extent)
        return lax.dynamic_update_index_in_dim(collected, updated, slot, 1)

    def one_pair(turn, collected):
        first_slot = slot_list[turn, 0]
        second_slot = slot_list[turn, 1]
        offset = offset_list[turn]
        first_box = fetch(first_slot)
        second_box = fetch(second_slot)
        shifted = shift_box(second_box, offset[0], offset[1], offset[2])
        potential = poisson(first_box * shifted, table, green)
        collected = add_slot(collected, first_slot, -(potential * shifted))
        returned = shift_box(-(potential * first_box), -offset[0], -offset[1], -offset[2])
        return add_slot(collected, second_slot, returned)

    start = jnp.zeros((extent, capacity, extent * extent), jnp.float32)
    collected = lax.fori_loop(jnp.int32(0), pair_total, one_pair, start)
    return collected.astype(jnp.bfloat16)


def shards(orbitals, box_list, pair_slots, offsets, pair_count):
    planes, orbital_total, row_cells = orbitals.shape
    grid_count, pair_workers, capacity = box_list.shape
    extent = planes * grid_count
    routing = jnp.transpose(box_list, (0, 2, 1)).reshape(-1)
    outgoing = jnp.take(orbitals, routing, axis=1)
    outgoing = outgoing.reshape(planes, grid_count, capacity, pair_workers, row_cells)
    row_pieces = lax.all_to_all(outgoing, "pair", split_axis=3, concat_axis=4, tiled=True)
    arrived = lax.all_to_all(row_pieces, "grid", split_axis=1, concat_axis=0, tiled=True)
    box_data = arrived.reshape(extent, capacity, extent * extent)
    fields = worker_fields(box_data, pair_slots[0, 0], offsets[0, 0], pair_count[0, 0])
    outbound = fields.reshape(extent, 1, capacity, 1, extent * extent)
    plane_pieces = lax.all_to_all(outbound, "grid", split_axis=0, concat_axis=1, tiled=True)
    landed = lax.all_to_all(plane_pieces, "pair", split_axis=4, concat_axis=3, tiled=True)
    pieces = jnp.moveaxis(landed.reshape(planes, -1, row_cells), 1, 0)
    summed = jax.ops.segment_sum(pieces.astype(jnp.float32), routing, num_segments=orbital_total)
    return jnp.moveaxis(summed, 0, 1)


def solution(mesh):
    placed = (
        P("grid", None, "pair"),
        P(),
        P("grid", "pair", None, None),
        P("grid", "pair", None, None),
        P("grid", "pair"),
    )
    return jax.shard_map(
        shards, mesh=mesh, in_specs=placed, out_specs=P("grid", None, "pair"), check_vma=False
    )
```

profile of v0, /device:TPU:0, one launch (start us, length us, event | category | flops | bytes accessed | tf_op | source)
XLA Modules:
  0.0 719.5 jit_solution(2379625165462570678)
XLA Ops:
  1.7 8.0 %gather_fusion = bf16[128,8,1024]{2,0,1:T(8,128)(2,1)} fusion(bf16[8,16,1024]{2,1,0:T(8,128)(2,1)S(1)} %copy-done, s32[1024]{0:T(1024)S(1)} %pad_clamp_fusion), kind=kCustom, calls=%fused_computation | custom fusion | bytes 4194816 | tf_op jit(solution)/shard_map/jit(_take)/gather | solution.py:83
  9.7 2.7 gather.7
  14.4 54.3 %all_to_all.54 = bf16[8,8,4,4,1024]{4,2,1,0,3:T(4,128)(2,1)S(1)} all-to-all(bf16[8,8,4,4,1024]{4,2,1,0,3:T(4,128)(2,1)S(1)} %copy_select_fusion), channel_id=1, replica_groups=mesh['grid'=8,'pair'=4] {'pair'}, dimensions={3} | all-to-all | bytes 4194304 | tf_op jit(solution)/shard_map/all_to_all | solution.py:85
  70.4 2.8 reshape.202
  73.2 3.9 all-to-all-start.1
  77.2 26.4 %all-to-all-done.1 = bf16[8,8,4,1,4096]{4,0,2,3,1:T(8,128)(2,1)S(1)} async-done(((bf16[8,8,4,1,4096]{4,0,2,3,1:T(8,128)(2,1)}), bf16[8,8,4,1,4096]{4,0,2,3,1:T(8,128)(2,1)S(1)}, u32[]{:S(2)}, u32[]{:S(2)}) %all-to-all-start.1) | async-done | bytes 2097184 | tf_op jit(solution)/shard_map/all_to_all | solution.py:86
  105.1 2.4 broadcast_in_dim.22
  107.6 293.5 %while.15 = (s32[]{:T(128)}, f32[64,4,4096]{2,0,1:T(8,128)}, s32[]{:T(128)}, s32[4,2]{0,1:T(2,128)S(1)}, bf16[64,4,4096]{2,0,1:T(8,128)(2,1)}, /*index=5*/s32[4,...) while((s32[]{:T(128)}, f32[64,4,4096]{2,0,1:T(8,128)}, ...), condition=%wide.region_1.2_spmd.clone.clone, body=%wide.region_0.1_spmd.clone.clone.sunk | while | flops 1211998208 | bytes 44581792 | solution.py:74
  142.1 5.7 fusion.90
  147.8 4.1 copy.118
  151.9 3.6 fusion.91
  155.5 3.9 divide_multiply_fusion.2
  159.5 5.7 fusion.92
  165.2 4.1 copy.119
  169.3 3.6 fusion.93
  172.9 6.0 multiply_negate_fusion.2
  181.1 2.5 add_dynamic-update-slice_fusion.4
  185.5 2.5 pad_dynamic-slice_fusion.3
  190.1 2.3 add_dynamic-update-slice_fusion.5
  208.2 5.7 fusion.90
  213.9 4.1 copy.118
  218.0 3.6 fusion.91
  221.6 3.9 divide_multiply_fusion.2
  225.6 5.7 fusion.92
  231.3 4.1 copy.119
  235.4 3.6 fusion.93
  239.0 6.0 multiply_negate_fusion.2
  247.2 2.5 add_dynamic-update-slice_fusion.4
  251.6 2.5 pad_dynamic-slice_fusion.3
  256.2 2.3 add_dynamic-update-slice_fusion.5
  274.3 5.7 fusion.90
  280.0 4.1 copy.118
  284.2 3.6 fusion.91
  287.8 3.9 divide_multiply_fusion.2
  291.7 5.7 fusion.92
  297.4 4.1 copy.119
  301.6 3.6 fusion.93
  305.2 6.0 multiply_negate_fusion.2
  313.3 2.5 add_dynamic-update-slice_fusion.4
  317.8 2.5 pad_dynamic-slice_fusion.3
  340.5 5.7 fusion.90
  346.2 4.1 copy.118
  350.4 3.6 fusion.91
  354.0 3.9 divide_multiply_fusion.2
  357.9 5.7 fusion.92
  363.6 4.1 copy.119
  367.7 3.6 fusion.93
  371.3 6.0 multiply_negate_fusion.2
  379.5 2.5 add_dynamic-update-slice_fusion.4
  383.9 2.5 pad_dynamic-slice_fusion.3
  388.6 2.3 add_dynamic-update-slice_fusion.5
  401.1 2.5 convert_element_type.87
  405.2 29.0 %all_to_all.55 = bf16[64,1,4,1,4096]{4,2,3,1,0:T(4,128)(2,1)S(1)} all-to-all(bf16[64,1,4,1,4096]{4,2,3,1,0:T(4,128)(2,1)S(1)} %bitcast.137), channel_id=1, replica_groups=mesh['grid'=8,'pair'=4] {'grid'}, dimensions={0} | all-to-all | bytes 4194304 | tf_op jit(solution)/shard_map/all_to_all | solution.py:90
  434.2 44.8 %copy.89 = bf16[8,8,1,4,1,4096]{0,1,3,5,4,2:T(8,128)(2,1)} copy(bf16[8,8,1,4,1,4096]{5,3,1,0,4,2:T(4,128)(2,1)S(1)} %bitcast.136) | data formatting | bytes 4194304 | tf_op jit(solution)/shard_map/all_to_all | solution.py:90
  479.0 22.1 %bitcast_bitcast_fusion = bf16[4096,4,1,8,8]{4,3,2,1,0:T(8,128)(2,1)} fusion(bf16[8,8,1,4,1,4096]{0,1,3,5,4,2:T(8,128)(2,1)} %copy.89), kind=kLoop, calls=%fused_computation.83 | loop fusion | bytes 4194304
  501.1 53.6 %reshape.203 = bf16[4,2,131072]{2,1,0:T(2,128)(2,1)} reshape(bf16[4096,4,1,8,8]{4,3,2,1,0:T(8,128)(2,1)} %bitcast_bitcast_fusion) | data formatting | bytes 4194304
  554.7 4.0 all-to-all-start.3
  558.8 47.7 %all-to-all-done.3 = bf16[4,2,131072]{2,1,0:T(2,128)(2,1)S(1)} async-done(((bf16[4,2,131072]{2,1,0:T(2,128)(2,1)}), bf16[4,2,131072]{2,1,0:T(2,128)(2,1)S(1)}, u32[]{:S(2)}, u32[]{:S(2)}) %all-to-all-start.3) | async-done | bytes 2097184 | tf_op jit(solution)/shard_map/all_to_all | solution.py:91
  606.5 52.2 %reshape.204 = bf16[4096,4,1,8,8]{4,3,2,1,0:T(8,128)(2,1)} reshape(bf16[4,2,131072]{2,1,0:T(2,128)(2,1)S(1)} %all-to-all-done.3) | data formatting | bytes 4194304
  658.7 29.4 %copy.90 = bf16[8,8,4,1,4096]{4,1,3,2,0:T(8,128)(2,1)S(1)} copy(bf16[8,8,4,1,4096]{1,0,3,2,4:T(8,128)(2,1)} %bitcast.133) | data formatting | bytes 4194304 | tf_op jit(solution)/shard_map/all_to_all | solution.py:91
  688.1 3.6 copy.91
  691.7 6.0 reshape.180
  697.7 6.6 copy.92
  704.4 13.5 %scatter_fusion = f32[16,8,1024]{2,1,0:T(8,128)S(1)} fusion(f32[16,8,1024]{2,1,0:T(8,128)S(1)} %broadcast_in_dim.21, s32[128]{0:T(128)S(1)} %reshape.191, f32[128,8,1024]{2,1,0:T(8,128)} %copy.92), kind=kCustom, calls=%fused_computation.1 | custom fusion | flops 1048576 | bytes 12583424 | tf_op jit(solution)/shard_map/scatter-add | solution.py:93
  (73 shorter events, 59.7 us)
Async XLA Ops:
  0.0 1.7 copy-start
  1.5 8.2 %copy-start.3 = (s32[8,4,4]{2,1,0:T(4,128)}, s32[8,4,4]{2,1,0:T(4,128)S(1)}, u32[]{:S(2)}) copy-start(s32[8,4,4]{2,1,0:T(4,128)S(1)} %copy.80) | copy-start | bytes 1540
  73.2 3.9 copy-start.6
  73.2 30.5 %all-to-all-start.1 = ((bf16[8,8,4,1,4096]{4,0,2,3,1:T(8,128)(2,1)}), bf16[8,8,4,1,4096]{4,0,2,3,1:T(8,128)(2,1)S(1)}, u32[]{:S(2)}, u32[]{:S(2)}) async-start(bf16[8,8,4,1,4096]{4,0,2,3,1:T(8,128)(2,1)} %reshape.202), calls=%async_computation.1 | async-start | bytes 4194304 | tf_op jit(solution)/shard_map/all_to_all | solution.py:86
  105.1 2.4 copy-start.5
  181.1 4.4 copy-start.2
  247.2 4.4 copy-start.2
  313.3 4.4 copy-start.2
  379.5 4.4 copy-start.2
  554.7 4.0 copy-start.4
  554.7 51.7 %all-to-all-start.3 = ((bf16[4,2,131072]{2,1,0:T(2,128)(2,1)}), bf16[4,2,131072]{2,1,0:T(2,128)(2,1)S(1)}, u32[]{:S(2)}, u32[]{:S(2)}) async-start(bf16[4,2,131072]{2,1,0:T(2,128)(2,1)} %reshape.203), calls=%async_computation.3 | async-start | bytes 4194304 | tf_op jit(solution)/shard_map/all_to_all | solution.py:91
  704.4 14.6 %copy-start.1 = (bf16[8,16,1024]{2,1,0:T(8,128)(2,1)S(1)}, bf16[8,16,1024]{2,1,0:T(8,128)(2,1)}, u32[]{:S(2)}) copy-start(bf16[8,16,1024]{2,1,0:T(8,128)(2,1)} %param.7) | copy-start | bytes 786436
where the time goes:
time: 731 us; the launch traced here: 719 us
  local copies, waits for them, and re-layouts  318 us (44%)
  matrix products  114 us (16%)
  blocking collectives  83.4 us (11%)
  waiting for transfers between devices  74.1 us (10%)
  loops' own time  69.3 us (9%)
  other arithmetic  52.1 us (7%)
  starting transfers between devices  7.8 us (1%)
    unnamed x17, local copies, waits for them, and re-layouts  130 us
    another operation x1, loops' own time, worker_fields(): collected = lax.fori_loop(jnp.int32(0), pair_total, one_pair, start)  69.3 us
    all_to_all x1, blocking collectives, shards(): lax.all_to_all(outgoing, 'pair', split_axis=3, concat_axis=4, tiled=True)  54.3 us
    all_to_all x1, waiting for transfers between devices, shards(): lax.all_to_all(plane_pieces, 'pair', split_axis=4, concat_axis=3, tiled=T...  47.7 us
    all_to_all x1, local copies, waits for them, and re-layouts, shards(): lax.all_to_all(outbound, 'grid', split_axis=0, concat_axis=1, tiled=True)  44.8 us
    all_to_all x1, local copies, waits for them, and re-layouts, shards(): lax.all_to_all(plane_pieces, 'pair', split_axis=4, concat_axis=3, tiled=T...  29.4 us
    all_to_all x1, blocking collectives, shards(): lax.all_to_all(outbound, 'grid', split_axis=0, concat_axis=1, tiled=True)  29 us
    dot_general x8, matrix products, poisson(): spectrum = jnp.einsum('by,ayz->abz', table, spectrum, precision=high)  28.7 us
  transfers between devices with their start and end apart: 2, of which 2 were waited for; matrix products, arithmetic and copies ran while one was open for 0% of the time, Pallas kernels for 0%

commit v1 on v0

v1 whole, which is shorter than its diff:
```python
import functools
import math

import jax
import jax.numpy as jnp
import ml_dtypes
import numpy as np
from jax import lax
from jax.experimental import pallas as pl
from jax.experimental.pallas import tpu as pltpu
from jax.sharding import PartitionSpec as P

SHIFT = 8
SCREENING = 0.02
F32 = jnp.float32
BF16 = jnp.bfloat16
VMEM_BYTES = 44 * 1024 * 1024


def split_np(values):
    high = values.astype(ml_dtypes.bfloat16)
    low = (values - high.astype(np.float64)).astype(ml_dtypes.bfloat16)
    return high, low


def stack_np(values, axis):
    high, low = split_np(values)
    return np.concatenate([high, high, low], axis=axis)


def tables(extent):
    half = extent // 2
    places = np.arange(extent)
    phases = (places[:, None] * places[None, :] % extent) * (2.0 * math.pi / extent)
    cas = np.cos(phases) + np.sin(phases)
    table_y = stack_np(cas, 1)
    parts = np.stack([cas[:half, xl::2] for xl in (0, 1)])
    ahead = stack_np(parts.reshape(extent, half), 1)
    back = stack_np(np.swapaxes(parts, 1, 2).reshape(extent, half), 1)
    butterfly = np.array([[1.0, 1.0], [1.0, -1.0]])
    table_z = stack_np(np.kron(butterfly, cas), 0)
    eigen = 2.0 - 2.0 * np.cos(places * (2.0 * math.pi / extent))
    denominator = SCREENING + eigen[:, None, None] + eigen[None, :, None] + eigen[None, None, :]
    green = -1.0 / (denominator * float(extent**3))
    green = green.reshape(2, half, extent, extent).transpose(2, 1, 0, 3)
    green = green.reshape(extent, half, 2 * extent).astype(np.float32)
    return table_y, ahead, back, table_z, green


def split(values):
    high = values.astype(BF16)
    return high, (values - high.astype(F32)).astype(BF16)


def three(values, axis):
    high, low = split(values)
    return jnp.concatenate([high, low, high], axis=axis)


def mul(left, right):
    return jnp.dot(left, right, preferred_element_type=F32)


def lane_low(extent):
    return lax.broadcasted_iota(jnp.int32, (1, 2 * extent), 1) < extent


def pieces_kernel(extent, slab, out, rows):
    planes, orbitals, cells = slab.shape
    heights = cells // extent
    wide = 2 * extent
    low = lane_low(extent)
    stride = (planes // 2) * heights
    for xh in range(planes // 2):
        for j in range(heights // 2):
            first = slab[2 * xh, :, j * wide : (j + 1) * wide].astype(F32)
            second = slab[2 * xh + 1, :, j * wide : (j + 1) * wide].astype(F32)
            even = jnp.where(low, first, pltpu.roll(second, extent, 1))
            odd = jnp.where(low, pltpu.roll(first, extent, 1), second)
            rows[pl.ds(xh * heights + 2 * j, orbitals, stride=stride), :] = even
            rows[pl.ds(xh * heights + 2 * j + 1, orbitals, stride=stride), :] = odd
    out[...] = rows[...].reshape(out.shape).astype(BF16)


def slab_kernel(extent, *refs):
    parts, out, rows = refs[:-2], refs[-2], refs[-1]
    planes, orbitals, cells = out.shape
    heights = cells // extent
    wide = 2 * extent
    low = lane_low(extent)
    stride = (planes // 2) * heights
    total = parts[0][...].astype(F32)
    for part in parts[1:]:
        total = total + part[...].astype(F32)
    rows[...] = total.reshape(rows.shape)
    for xh in range(planes // 2):
        for j in range(heights // 2):
            even = rows[pl.ds(xh * heights + 2 * j, orbitals, stride=stride), :]
            odd = rows[pl.ds(xh * heights + 2 * j + 1, orbitals, stride=stride), :]
            first = jnp.where(low, even, pltpu.roll(odd, extent, 1))
            second = jnp.where(low, pltpu.roll(even, extent, 1), odd)
            out[2 * xh, :, j * wide : (j + 1) * wide] = first
            out[2 * xh + 1, :, j * wide : (j + 1) * wide] = second


def choose_kernel(pair_total, grid_total, capacity, place, boxes, *refs):
    parts, outs = refs[:pair_total], refs[pair_total:]
    me, mate = place[0], place[1]
    for turn, out in enumerate(outs):
        target = lax.bitwise_xor(me, turn)
        for slot in range(capacity):
            orbital = boxes[(target * pair_total + mate) * capacity + slot]
            for step, part in enumerate(parts):
                out[slot, :, lax.bitwise_xor(mate, step)] = part[orbital]


def gather_kernel(pair_total, grid_total, capacity, place, boxes, *refs):
    parts, outs, total = refs[:grid_total], refs[grid_total:-1], refs[-1]
    me, mate = place[0], place[1]
    total[...] = jnp.zeros_like(total)
    for turn, part in enumerate(parts):
        origin = lax.bitwise_xor(me, turn)
        for slot in range(capacity):
            orbital = boxes[(origin * pair_total + mate) * capacity + slot]
            total[orbital] += part[slot].astype(F32)
    for step, out in enumerate(outs):
        out[...] = total[:, :, lax.bitwise_xor(mate, step)].astype(out.dtype)


def worker_kernel(extent, grid_total, place, slots, offsets, count, *refs):
    parts = refs[:grid_total]
    table_y, ahead, back, table_z, green = refs[grid_total : grid_total + 5]
    outs = refs[grid_total + 5 : 2 * grid_total + 5]
    box, shifted, first, second, returned, collected = refs[2 * grid_total + 5 :]
    capacity, local, pair_total, heights, wide = parts[0].shape
    half = extent // 2
    edge = SHIFT // 2
    me = place[0]
    low = lane_low(extent)
    lanes = lax.broadcasted_iota(jnp.int32, (1, wide), 1)
    depth = lanes - jnp.where(low, 0, extent)

    def clear(ref):
        blank = jnp.zeros((SHIFT, wide), F32)
        def one(index, carry):
            ref[index, :SHIFT] = blank
            ref[index, SHIFT + extent :] = blank
            return carry
        lax.fori_loop(0, ref.shape[0], one, 0)
        for index in (*range(edge), *range(edge + half, ref.shape[0])):
            ref[index] = jnp.zeros(ref.shape[1:], F32)

    clear(returned)
    for slot in range(capacity):
        clear(box.at[slot])
    for turn, part in enumerate(parts):
        start = edge + lax.bitwise_xor(me, turn) * local
        for slot in range(capacity):
            for xh in range(local):
                for p in range(pair_total):
                    box[slot, start + xh, SHIFT + p * heights : SHIFT + (p + 1) * heights] = part[
                        slot, xh, p
                    ].astype(F32)

    def moved(ref, xh, steps):
        step_x, step_y, step_z = steps
        odd = lax.bitwise_and(step_x, 1)
        near = edge + xh + lax.shift_right_arithmetic(step_x, 1)
        rows = pl.ds(SHIFT + step_y, extent)
        upper = ref[near, rows, :]
        lower = ref[near + odd, rows, :]
        joined = jnp.where(low, lower, upper)
        amount = lax.rem(2 * wide - odd * extent - step_z, wide)
        rolled = pltpu.roll(joined, amount, 1)
        kept = jnp.logical_and(depth + step_z >= 0, depth + step_z < extent)
        return jnp.where(kept, rolled, 0.0)

    def one_pair(turn, fresh):
        slot_a, slot_b = slots[2 * turn], slots[2 * turn + 1]
        steps = tuple(offsets[3 * turn + i] for i in range(3))
        opposite = tuple(-s for s in steps)

        def load_y(group, carry):
            for pair in range(2):
                stacks = []
                for member in range(2):
                    xh = group * 4 + pair * 2 + member
                    other = moved(box.at[slot_b], xh, steps)
                    shifted[xh] = other
                    own = box[slot_a, edge + xh, SHIFT : SHIFT + extent]
                    stacks.append(three(own * other, 0))
                done = mul(table_y[...], jnp.concatenate(stacks, axis=1))
                for member in range(2):
                    xh = group * 4 + pair * 2 + member
                    first[pl.ds(pl.multiple_of(xh * extent, extent), extent), :] = done[
                        :, member * wide : (member + 1) * wide
                    ]
            return carry

        lax.fori_loop(0, half // 4, load_y, 0)

        many = 8

        def middle(group, carry):
            def apply_x(table, values):
                results = []
                for pair in range(many // 2):
                    stack = jnp.concatenate([three(v, 0) for v in values[2 * pair : 2 * pair + 2]], axis=1)
                    done = mul(table[...], stack)
                    for member in range(2):
                        piece = done[:, member * wide : (member + 1) * wide]
                        results.append(jnp.where(low, piece[:half], piece[half:]))
                return results

            values = [
                first[pl.ds(group * many + i, half, stride=extent), :] for i in range(many)
            ]
            spectrum = jnp.concatenate(apply_x(ahead, values), axis=0)
            spectrum = mul(three(spectrum, 1), table_z[...])
            weights = green[pl.ds(group * many, many)].reshape(many * half, wide)
            spectrum = mul(three(spectrum * weights, 1), table_z[...])
            values = [spectrum[i * half : (i + 1) * half] for i in range(many)]
            for i, value in enumerate(apply_x(back, values)):
                second[pl.ds(group * many + i, half, stride=extent), :] = value
            return carry

        lax.fori_loop(0, extent // many, middle, 0)

        def unload_y(group, carry):
            for pair in range(2):
                stacks = []
                for member in range(2):
                    xh = group * 4 + pair * 2 + member
                    rows = pl.ds(pl.multiple_of(xh * extent, extent), extent)
                    stacks.append(three(second[rows, :], 0))
                done = mul(table_y[...], jnp.concatenate(stacks, axis=1))
                for member in range(2):
                    xh = group * 4 + pair * 2 + member
                    potential = done[:, member * wide : (member + 1) * wide]
                    value = potential * shifted[xh]
                    if fresh:
                        collected[slot_a, xh] = value
                    else:
                        collected[slot_a, xh] += value
                    own = box[slot_a, edge + xh, SHIFT : SHIFT + extent]
                    returned[edge + xh, SHIFT : SHIFT + extent] = potential * own
            return carry

        lax.fori_loop(0, half // 4, unload_y, 0)

        def give(group, carry):
            for member in range(4):
                xh = group * 4 + member
                value = moved(returned, xh, opposite)
                if fresh:
                    collected[slot_b, xh] = value
                else:
                    collected[slot_b, xh] += value
            return carry

        lax.fori_loop(0, half // 4, give, 0)

    def opening(turn, carry):
        one_pair(turn, True)
        return carry

    def later(turn, carry):
        one_pair(turn, False)
        return carry

    lax.fori_loop(0, capacity // 2, opening, 0)
    lax.fori_loop(capacity // 2, count[0], later, 0)

    for turn, out in enumerate(outs):
        start = lax.bitwise_xor(me, turn) * local
        for slot in range(capacity):
            for xh in range(local):
                for p in range(pair_total):
                    out[slot, xh, p] = collected[
                        slot, start + xh, p * heights : (p + 1) * heights
                    ].astype(BF16)


def spec(count):
    return [pl.BlockSpec(memory_space=pltpu.VMEM)] * count


def scalars(count):
    return [pl.BlockSpec(memory_space=pltpu.SMEM)] * count


def call(kernel, scalar_count, inputs, out_shapes, scratch, flops=0):
    moved = sum(math.prod(a.shape) * a.dtype.itemsize for a in (*inputs, *out_shapes))
    return pl.pallas_call(
        kernel,
        out_shape=out_shapes,
        in_specs=scalars(scalar_count) + spec(len(inputs) - scalar_count),
        out_specs=spec(len(out_shapes)),
        scratch_shapes=scratch,
        compiler_params=pltpu.CompilerParams(vmem_limit_bytes=VMEM_BYTES),
        cost_estimate=pl.CostEstimate(flops=flops, bytes_accessed=moved, transcendentals=0),
    )(*inputs)


def swap(arrays, axis, total):
    return [
        array if k == 0 else lax.ppermute(array, axis, [(i, i ^ k) for i in range(total)])
        for k, array in enumerate(arrays)
    ]


def shards(grid_total, pair_total, orbitals, box_list, pair_slots, offsets, pair_count):
    planes, orbital_total, cells = orbitals.shape
    capacity = box_list.shape[2]
    extent = planes * grid_total
    heights = cells // extent
    local, half, wide = planes // 2, extent // 2, 2 * extent
    padded_x, padded_y = half + SHIFT + 1, extent + 2 * SHIFT
    place = jnp.stack([lax.axis_index("grid"), lax.axis_index("pair")]).astype(jnp.int32)
    boxes = box_list.reshape(-1)
    shape = jax.ShapeDtypeStruct

    piece = (orbital_total, local, heights, wide)
    rows = pltpu.VMEM((math.prod(piece[:-1]), wide), F32)
    bundle = (capacity, local, pair_total, heights, wide)

    (own,) = call(functools.partial(pieces_kernel, extent), 0, [orbitals], [shape(piece, BF16)], [rows])
    gathered = swap([own] * pair_total, "pair", pair_total)
    outgoing = call(
        functools.partial(choose_kernel, pair_total, grid_total, capacity),
        2,
        [place, boxes, *gathered],
        [shape(bundle, BF16)] * grid_total,
        [],
    )
    arrived = swap(outgoing, "grid", grid_total)
    fields = call(
        functools.partial(worker_kernel, extent, grid_total),
        4,
        [
            place,
            pair_slots.reshape(-1),
            offsets.reshape(-1),
            pair_count.reshape(-1),
            *arrived,
            *(jnp.asarray(t) for t in tables(extent)),
        ],
        [shape(bundle, BF16)] * grid_total,
        [
            pltpu.VMEM((capacity, padded_x, padded_y, wide), F32),
            pltpu.VMEM((half, extent, wide), F32),
            pltpu.VMEM((half * extent, wide), F32),
            pltpu.VMEM((half * extent, wide), F32),
            pltpu.VMEM((padded_x, padded_y, wide), F32),
            pltpu.VMEM((capacity, half, extent, wide), F32),
        ],
        flops=3 * 2 * 6 * 3 * extent**4,
    )
    landed = swap(fields, "grid", grid_total)
    sums = call(
        functools.partial(gather_kernel, pair_total, grid_total, capacity),
        2,
        [place, boxes, *landed],
        [shape(piece, F32)] + [shape(piece, BF16)] * (pair_total - 1),
        [pltpu.VMEM((orbital_total, local, pair_total, heights, wide), F32)],
    )
    parts = swap(sums, "pair", pair_total)
    (result,) = call(
        functools.partial(slab_kernel, extent), 0, parts, [shape(orbitals.shape, F32)], [rows]
    )
    return result


def solution(mesh):
    placed = (
        P("grid", None, "pair"),
        P(),
        P("grid", "pair", None, None),
        P("grid", "pair", None, None),
        P("grid", "pair"),
    )
    body = functools.partial(shards, mesh.shape["grid"], mesh.shape["pair"])
    return jax.shard_map(
        body, mesh=mesh, in_specs=placed, out_specs=P("grid", None, "pair"), check_vma=False
    )
```

time: 731 us -> 154 us (0.21); the launches traced: 719 us -> 151 us
  local copies, waits for them, and re-layouts: 318 us -> 4.08 us
  matrix products: 114 us -> 0 us
  blocking collectives: 83.4 us -> 0 us
  loops' own time: 69.3 us -> 0 us
  other arithmetic: 52.1 us -> 0.08 us
  Pallas kernels: 0 us -> 35.5 us
  starting transfers between devices: 7.8 us -> 35 us
    unnamed x17 -> x21, local copies, waits for them, and re-layouts: 130 us -> 3.8 us
    dot_general x24 -> x0, matrix products: 114 us -> none  [the longest x8 28.7 us: poisson(): spectrum = jnp.einsum('by,ayz->abz', table, spectrum, precision=high)]
    all_to_all x2 -> x0, blocking collectives: 83.4 us -> none  [the longest x1 54.3 us: shards(): lax.all_to_all(outgoing, 'pair', split_axis=3, concat_axis=4, tiled=True)]
    all_to_all x5 -> x0, local copies, waits for them, and re-layouts: 80.1 us -> none  [the longest x1 44.8 us: shards(): lax.all_to_all(outbound, 'grid', split_axis=0, concat_axis=1, tiled=True)]
    ppermute x0 -> x20, waiting for transfers between devices: none -> 75.4 us  [swap(): lax.ppermute(array, axis, [(i, i ^ k) for i in range(total)])]
    all_to_all x2 -> x0, waiting for transfers between devices: 74.1 us -> none  [the longest x1 47.7 us: shards(): lax.all_to_all(plane_pieces, 'pair', split_axis=4, concat_axis=3, tiled=T...]
    another operation x1 -> x0, loops' own time: 69.3 us -> none  [worker_fields(): collected = lax.fori_loop(jnp.int32(0), pair_total, one_pair, start)]
    pallas_call x0 -> x5, Pallas kernels: none -> 35.5 us  [call(): pl.pallas_call(kernel, out_shape=out_shapes, in_specs=scalars(scalar_coun...]
  transfers between devices with their start and end apart: 2 -> 20, of which waited for: 2 -> 10; matrix products, arithmetic and copies ran while one was open for 0% -> 0% of each run, Pallas kernels for 0% -> 0%
where the time goes in v1:
time: 154 us; the launch traced here: 151 us
  waiting for transfers between devices  75.4 us (49%)
  Pallas kernels  35.5 us (23%)
  starting transfers between devices  35 us (23%)
  local copies, waits for them, and re-layouts  4.08 us (3%)
    ppermute x20, waiting for transfers between devices, swap(): lax.ppermute(array, axis, [(i, i ^ k) for i in range(total)])  75.4 us
    pallas_call x5, Pallas kernels, call(): pl.pallas_call(kernel, out_shape=out_shapes, in_specs=scalars(scalar_coun...  35.5 us
    ppermute x20, starting transfers between devices, swap(): lax.ppermute(array, axis, [(i, i ^ k) for i in range(total)])  35 us
    unnamed x21, local copies, waits for them, and re-layouts  3.8 us
  transfers between devices with their start and end apart: 20, of which 10 were waited for; matrix products, arithmetic and copies ran while one was open for 0% of the time, Pallas kernels for 0%

profile of v1, /device:TPU:0, one launch (start us, length us, event | category | flops | bytes accessed | tf_op | source)
XLA Modules:
  0.0 150.8 jit_solution(11924957508261109362)
XLA Ops:
  0.0 0.9 copy-done
  1.0 0.5 shard_map.100.refs_0_
  1.5 0.0 copy-start.6
  1.5 5.1 %collective-permute-start.2 = (bf16[16,4,16,128]{3,2,1,0:T(8,128)(2,1)S(1)}, bf16[16,4,16,128]{3,2,1,0:T(8,128)(2,1)S(1)}, u32[]{:S(2)}, u32[]{:S(2)}) collective-permute-start(bf16[16,4,16,128]{3,2,1,0:T(8,128)(2,1)S(1)} %shard_map.100.refs_0_), channel_id=1, source_target_pairs={{0,3},{1,2},{2,1},{3,0},{4,7},{5,6},{6,5},{7,4},{8,11},{9,10},{10,... | collective-permute-start | bytes 786440 | tf_op jit(solution)/shard_map/ppermute | solution.py:307
  6.6 0.0 collective-permute-start.1
  6.6 0.6 collective-permute-start
  7.2 0.0 copy-done.6
  7.2 0.1 copy.14
  7.3 0.1 reshape.12.boxes
  7.5 0.1 pad_add_fusion.place
  7.5 6.3 %collective-permute-done.2.refs_3_ = bf16[16,4,16,128]{3,2,1,0:T(8,128)(2,1)S(1)} collective-permute-done((bf16[16,4,16,128]{3,2,1,0:T(8,128)(2,1)S(1)}, bf16[16,4,16,128]{3,2,1,0:T(8,128)(2,1)S(1)}, u32[]{:S(2)}, u32[]{:S(2)}) %collective-permute-start.2) | collective-permute-done | bytes 262176 | tf_op jit(solution)/shard_map/ppermute | solution.py:307
  13.9 15.0 %collective-permute-done.1.refs_2_ = bf16[16,4,16,128]{3,2,1,0:T(8,128)(2,1)S(1)} collective-permute-done((bf16[16,4,16,128]{3,2,1,0:T(8,128)(2,1)S(1)}, bf16[16,4,16,128]{3,2,1,0:T(8,128)(2,1)S(1)}, u32[]{:S(2)}, u32[]{:S(2)}) %collective-permute-start.1) | collective-permute-done | bytes 262176 | tf_op jit(solution)/shard_map/ppermute | solution.py:307
  28.9 0.0 collective-permute-done.refs_1_
  28.9 0.9 shard_map.101
  29.8 0.0 copy-start.4
  29.8 0.1 collective-permute-start.3
  29.9 1.6 %collective-permute-start.4 = (bf16[4,4,4,16,128]{4,3,2,1,0:T(8,128)(2,1)S(1)}, bf16[4,4,4,16,128]{4,3,2,1,0:T(8,128)(2,1)S(1)}, u32[]{:S(2)}, u32[]{:S(2)}) collective-permute-start(bf16[4,4,4,16,128]{4,3,2,1,0:T(8,128)(2,1)S(1)} %get-tuple-element.27), channel_id=1, source_target_pairs={{0,8},{4,12},{8,0},{12,4},{16,24},{20,28},{24,16},{28,20},{1,9},{5... | collective-permute-start | bytes 786440 | tf_op jit(solution)/shard_map/ppermute | solution.py:307
  31.4 0.3 collective-permute-start.5
  31.7 1.5 %collective-permute-start.6 = (bf16[4,4,4,16,128]{4,3,2,1,0:T(8,128)(2,1)S(1)}, bf16[4,4,4,16,128]{4,3,2,1,0:T(8,128)(2,1)S(1)}, u32[]{:S(2)}, u32[]{:S(2)}) collective-permute-start(bf16[4,4,4,16,128]{4,3,2,1,0:T(8,128)(2,1)S(1)} %get-tuple-element.29), channel_id=1, source_target_pairs={{0,16},{4,20},{8,24},{12,28},{16,0},{20,4},{24,8},{28,12},{1,17},{... | collective-permute-start | bytes 786440 | tf_op jit(solution)/shard_map/ppermute | solution.py:307
  33.3 0.2 collective-permute-start.7
  33.4 0.0 collective-permute-done.3.refs_1_
  33.4 2.4 %collective-permute-start.8 = (bf16[4,4,4,16,128]{4,3,2,1,0:T(8,128)(2,1)S(1)}, bf16[4,4,4,16,128]{4,3,2,1,0:T(8,128)(2,1)S(1)}, u32[]{:S(2)}, u32[]{:S(2)}) collective-permute-start(bf16[4,4,4,16,128]{4,3,2,1,0:T(8,128)(2,1)S(1)} %get-tuple-element.31), channel_id=1, source_target_pairs={{0,24},{4,28},{8,16},{12,20},{16,8},{20,12},{24,0},{28,4},{1,25},{... | collective-permute-start | bytes 786440 | tf_op jit(solution)/shard_map/ppermute | solution.py:307
  35.9 3.2 %collective-permute-done.4.refs_2_ = bf16[4,4,4,16,128]{4,3,2,1,0:T(8,128)(2,1)S(1)} collective-permute-done((bf16[4,4,4,16,128]{4,3,2,1,0:T(8,128)(2,1)S(1)}, bf16[4,4,4,16,128]{4,3,2,1,0:T(8,128)(2,1)S(1)}, u32[]{:S(2)}, u32[]{:S(2)}) %collective-permute-start.4) | collective-permute-done | bytes 262176 | tf_op jit(solution)/shard_map/ppermute | solution.py:307
  39.1 1.3 collective-permute-start.9
  41.0 0.0 copy-done.8
  41.0 0.1 copy.15
  41.1 0.1 reshape.13.slots
  41.2 0.6 copy-done.7
  41.8 0.1 copy.16
  41.8 0.1 reshape.14.offsets
  41.9 1.8 %collective-permute-done.5.refs_3_ = bf16[4,4,4,16,128]{4,3,2,1,0:T(8,128)(2,1)S(1)} collective-permute-done((bf16[4,4,4,16,128]{4,3,2,1,0:T(8,128)(2,1)S(1)}, bf16[4,4,4,16,128]{4,3,2,1,0:T(8,128)(2,1)S(1)}, u32[]{:S(2)}, u32[]{:S(2)}) %collective-permute-start.5) | collective-permute-done | bytes 262176 | tf_op jit(solution)/shard_map/ppermute | solution.py:307
  43.8 0.0 collective-permute-done.6.refs_4_
  43.8 12.8 %collective-permute-done.7.refs_5_ = bf16[4,4,4,16,128]{4,3,2,1,0:T(8,128)(2,1)S(1)} collective-permute-done((bf16[4,4,4,16,128]{4,3,2,1,0:T(8,128)(2,1)S(1)}, bf16[4,4,4,16,128]{4,3,2,1,0:T(8,128)(2,1)S(1)}, u32[]{:S(2)}, u32[]{:S(2)}) %collective-permute-start.7) | collective-permute-done | bytes 262176 | tf_op jit(solution)/shard_map/ppermute | solution.py:307
  56.6 0.0 collective-permute-done.8.refs_6_
  56.6 0.0 collective-permute-done.9.refs_7_
  56.6 0.0 copy-done.2
  56.6 0.0 copy-done.3
  56.6 0.0 copy-done.4
  56.6 0.0 copy-start.1
  56.6 1.2 copy-done.1
  57.9 0.7 copy-done.5
  58.6 31.6 %shard_map.102 = (bf16[4,4,4,16,128]{4,3,2,1,0:T(8,128)(2,1)S(1)}, bf16[4,4,4,16,128]{4,3,2,1,0:T(8,128)(2,1)S(1)}, bf16[4,4,4,16,128]{4,3,2,1,0:T(8,128)(2,1)S(...) custom-call(s32[2]{0:T(128)S(1)} %pad_add_fusion.place, ...), custom_call_target="tpu_custom_call" | custom-call | flops 1811939328 | bytes 5390428 | tf_op jit(solution)/shard_map/pallas_call | solution.py:294
  90.1 0.1 collective-permute-start.10
  90.2 11.0 %collective-permute-start.11 = (bf16[4,4,4,16,128]{4,3,2,1,0:T(8,128)(2,1)S(1)}, bf16[4,4,4,16,128]{4,3,2,1,0:T(8,128)(2,1)S(1)}, u32[]{:S(2)}, u32[]{:S(2)}) collective-permute-start(bf16[4,4,4,16,128]{4,3,2,1,0:T(8,128)(2,1)S(1)} %get-tuple-element.35), channel_id=1, source_target_pairs={{0,8},{4,12},{8,0},{12,4},{16,24},{20,28},{24,16},{28,20},{1,9},{5... | collective-permute-start | bytes 786440 | tf_op jit(solution)/shard_map/ppermute | solution.py:307
  101.2 0.1 collective-permute-start.12
  101.3 1.7 %collective-permute-start.13 = (bf16[4,4,4,16,128]{4,3,2,1,0:T(8,128)(2,1)S(1)}, bf16[4,4,4,16,128]{4,3,2,1,0:T(8,128)(2,1)S(1)}, u32[]{:S(2)}, u32[]{:S(2)}) collective-permute-start(bf16[4,4,4,16,128]{4,3,2,1,0:T(8,128)(2,1)S(1)} %get-tuple-element.37), channel_id=1, source_target_pairs={{0,16},{4,20},{8,24},{12,28},{16,0},{20,4},{24,8},{28,12},{1,17},{... | collective-permute-start | bytes 786440 | tf_op jit(solution)/shard_map/ppermute | solution.py:307
  103.0 0.3 collective-permute-start.14
  103.4 0.0 collective-permute-done.10.refs_1_
  103.4 2.4 %collective-permute-start.15 = (bf16[4,4,4,16,128]{4,3,2,1,0:T(8,128)(2,1)S(1)}, bf16[4,4,4,16,128]{4,3,2,1,0:T(8,128)(2,1)S(1)}, u32[]{:S(2)}, u32[]{:S(2)}) collective-permute-start(bf16[4,4,4,16,128]{4,3,2,1,0:T(8,128)(2,1)S(1)} %get-tuple-element.39), channel_id=1, source_target_pairs={{0,24},{4,28},{8,16},{12,20},{16,8},{20,12},{24,0},{28,4},{1,25},{... | collective-permute-start | bytes 786440 | tf_op jit(solution)/shard_map/ppermute | solution.py:307
  105.8 2.6 %collective-permute-done.11.refs_2_ = bf16[4,4,4,16,128]{4,3,2,1,0:T(8,128)(2,1)S(1)} collective-permute-done((bf16[4,4,4,16,128]{4,3,2,1,0:T(8,128)(2,1)S(1)}, bf16[4,4,4,16,128]{4,3,2,1,0:T(8,128)(2,1)S(1)}, u32[]{:S(2)}, u32[]{:S(2)}) %collective-permute-start.11) | collective-permute-done | bytes 262176 | tf_op jit(solution)/shard_map/ppermute | solution.py:307
  108.4 1.8 %collective-permute-start.16 = (bf16[4,4,4,16,128]{4,3,2,1,0:T(8,128)(2,1)S(1)}, bf16[4,4,4,16,128]{4,3,2,1,0:T(8,128)(2,1)S(1)}, u32[]{:S(2)}, u32[]{:S(2)}) collective-permute-start(bf16[4,4,4,16,128]{4,3,2,1,0:T(8,128)(2,1)S(1)} %get-tuple-element.40), channel_id=1, source_target_pairs={{0,28},{4,24},{8,20},{12,16},{16,12},{20,8},{24,4},{28,0},{1,29},{... | collective-permute-start | bytes 786440 | tf_op jit(solution)/shard_map/ppermute | solution.py:307
  110.2 3.3 %collective-permute-done.12.refs_3_ = bf16[4,4,4,16,128]{4,3,2,1,0:T(8,128)(2,1)S(1)} collective-permute-done((bf16[4,4,4,16,128]{4,3,2,1,0:T(8,128)(2,1)S(1)}, bf16[4,4,4,16,128]{4,3,2,1,0:T(8,128)(2,1)S(1)}, u32[]{:S(2)}, u32[]{:S(2)}) %collective-permute-start.12) | collective-permute-done | bytes 262176 | tf_op jit(solution)/shard_map/ppermute | solution.py:307
  113.5 0.0 collective-permute-done.13.refs_4_
  113.5 13.3 %collective-permute-done.14.refs_5_ = bf16[4,4,4,16,128]{4,3,2,1,0:T(8,128)(2,1)S(1)} collective-permute-done((bf16[4,4,4,16,128]{4,3,2,1,0:T(8,128)(2,1)S(1)}, bf16[4,4,4,16,128]{4,3,2,1,0:T(8,128)(2,1)S(1)}, u32[]{:S(2)}, u32[]{:S(2)}) %collective-permute-start.14) | collective-permute-done | bytes 262176 | tf_op jit(solution)/shard_map/ppermute | solution.py:307
  126.7 0.0 collective-permute-done.15.refs_6_
  126.7 0.0 collective-permute-done.16.refs_7_
  126.7 1.2 shard_map.103
  128.0 0.1 collective-permute-start.17
  128.1 0.1 collective-permute-start.18
  128.1 4.3 %collective-permute-start.19 = (bf16[16,4,16,128]{3,2,1,0:T(8,128)(2,1)S(1)}, bf16[16,4,16,128]{3,2,1,0:T(8,128)(2,1)S(1)}, u32[]{:S(2)}, u32[]{:S(2)}) collective-permute-start(bf16[16,4,16,128]{3,2,1,0:T(8,128)(2,1)S(1)} %get-tuple-element.44), channel_id=1, source_target_pairs={{0,3},{1,2},{2,1},{3,0},{4,7},{5,6},{6,5},{7,4},{8,11},{9,10},{10,... | collective-permute-start | bytes 786440 | tf_op jit(solution)/shard_map/ppermute | solution.py:307
  132.4 7.4 %collective-permute-done.17.refs_1_ = bf16[16,4,16,128]{3,2,1,0:T(8,128)(2,1)S(1)} collective-permute-done((bf16[16,4,16,128]{3,2,1,0:T(8,128)(2,1)S(1)}, bf16[16,4,16,128]{3,2,1,0:T(8,128)(2,1)S(1)}, u32[]{:S(2)}, u32[]{:S(2)}) %collective-permute-start.17) | collective-permute-done | bytes 262176 | tf_op jit(solution)/shard_map/ppermute | solution.py:307
  139.8 9.6 %collective-permute-done.18.refs_2_ = bf16[16,4,16,128]{3,2,1,0:T(8,128)(2,1)S(1)} collective-permute-done((bf16[16,4,16,128]{3,2,1,0:T(8,128)(2,1)S(1)}, bf16[16,4,16,128]{3,2,1,0:T(8,128)(2,1)S(1)}, u32[]{:S(2)}, u32[]{:S(2)}) %collective-permute-start.18) | collective-permute-done | bytes 262176 | tf_op jit(solution)/shard_map/ppermute | solution.py:307
  149.5 0.0 collective-permute-done.19.refs_3_
  149.5 1.3 shard_map.104
  (6 shorter events, 0.0 us)
Async XLA Ops:
  0.0 0.9 copy-start
  1.5 5.8 %copy-start.6 = (s32[8,4,4]{0,2,1:T(4,128)S(1)}, s32[8,4,4]{0,2,1:T(4,128)}, u32[]{:S(2)}) copy-start(s32[8,4,4]{0,2,1:T(4,128)} %param.11) | copy-start | bytes 1540
  1.5 12.4 %collective-permute-start.2 = (bf16[16,4,16,128]{3,2,1,0:T(8,128)(2,1)S(1)}, bf16[16,4,16,128]{3,2,1,0:T(8,128)(2,1)S(1)}, u32[]{:S(2)}, u32[]{:S(2)}) collective-permute-start(bf16[16,4,16,128]{3,2,1,0:T(8,128)(2,1)S(1)} %shard_map.100.refs_0_), channel_id=1, source_target_pairs={{0,3},{1,2},{2,1},{3,0},{4,7},{5,6},{6,5},{7,4},{8,11},{9,10},{10,... | collective-permute-start | bytes 786440 | tf_op jit(solution)/shard_map/ppermute | solution.py:307
  6.6 22.3 %collective-permute-start.1 = (bf16[16,4,16,128]{3,2,1,0:T(8,128)(2,1)S(1)}, bf16[16,4,16,128]{3,2,1,0:T(8,128)(2,1)S(1)}, u32[]{:S(2)}, u32[]{:S(2)}) collective-permute-start(bf16[16,4,16,128]{3,2,1,0:T(8,128)(2,1)S(1)} %shard_map.100.refs_0_), channel_id=1, source_target_pairs={{0,2},{1,3},{2,0},{3,1},{4,6},{5,7},{6,4},{7,5},{8,10},{9,11},{10,... | collective-permute-start | bytes 786440 | tf_op jit(solution)/shard_map/ppermute | solution.py:307
  6.6 22.3 %collective-permute-start = (bf16[16,4,16,128]{3,2,1,0:T(8,128)(2,1)S(1)}, bf16[16,4,16,128]{3,2,1,0:T(8,128)(2,1)S(1)}, u32[]{:S(2)}, u32[]{:S(2)}) collective-permute-start(bf16[16,4,16,128]{3,2,1,0:T(8,128)(2,1)S(1)} %shard_map.100.refs_0_), channel_id=1, source_target_pairs={{0,1},{1,0},{2,3},{3,2},{4,5},{5,4},{6,7},{7,6},{8,9},{9,8},{10,11... | collective-permute-start | bytes 786440 | tf_op jit(solution)/shard_map/ppermute | solution.py:307
  7.5 49.1 %copy-start.2 = (bf16[384,128]{1,0:T(8,128)(2,1)S(1)}, bf16[384,128]{1,0:T(8,128)(2,1)}, u32[]{:S(2)}) copy-start(bf16[384,128]{1,0:T(8,128)(2,1)} %constant.22.clone.refs_11_) | copy-start | bytes 294916
  7.5 49.1 %copy-start.3 = (bf16[64,192]{1,0:T(8,128)(2,1)S(1)}, bf16[64,192]{1,0:T(8,128)(2,1)}, u32[]{:S(2)}) copy-start(bf16[64,192]{1,0:T(8,128)(2,1)} %constant.19.clone.refs_8_) | copy-start | bytes 73732
  28.9 12.1 %copy-start.8 = (s32[1,1,4,2]{2,3,1,0:T(2,128)S(1)}, s32[1,1,4,2]{2,3,1,0:T(2,128)}, u32[]{:S(2)}) copy-start(s32[1,1,4,2]{2,3,1,0:T(2,128)} %param.12) | copy-start | bytes 100
  29.8 26.8 %copy-start.4 = (bf16[64,96]{1,0:T(8,128)(2,1)S(1)}, bf16[64,96]{1,0:T(8,128)(2,1)}, u32[]{:S(2)}) copy-start(bf16[64,96]{1,0:T(8,128)(2,1)} %constant.21.clone.refs_10_) | copy-start | bytes 36868
  29.8 3.6 %collective-permute-start.3 = (bf16[4,4,4,16,128]{4,3,2,1,0:T(8,128)(2,1)S(1)}, bf16[4,4,4,16,128]{4,3,2,1,0:T(8,128)(2,1)S(1)}, u32[]{:S(2)}, u32[]{:S(2)}) collective-permute-start(bf16[4,4,4,16,128]{4,3,2,1,0:T(8,128)(2,1)S(1)} %get-tuple-element.26), channel_id=1, source_target_pairs={{0,4},{4,0},{8,12},{12,8},{16,20},{20,16},{24,28},{28,24},{1,5},{5... | collective-permute-start | bytes 786440 | tf_op jit(solution)/shard_map/ppermute | solution.py:307
  29.9 9.2 %collective-permute-start.4 = (bf16[4,4,4,16,128]{4,3,2,1,0:T(8,128)(2,1)S(1)}, bf16[4,4,4,16,128]{4,3,2,1,0:T(8,128)(2,1)S(1)}, u32[]{:S(2)}, u32[]{:S(2)}) collective-permute-start(bf16[4,4,4,16,128]{4,3,2,1,0:T(8,128)(2,1)S(1)} %get-tuple-element.27), channel_id=1, source_target_pairs={{0,8},{4,12},{8,0},{12,4},{16,24},{20,28},{24,16},{28,20},{1,9},{5... | collective-permute-start | bytes 786440 | tf_op jit(solution)/shard_map/ppermute | solution.py:307
  31.4 12.3 %collective-permute-start.5 = (bf16[4,4,4,16,128]{4,3,2,1,0:T(8,128)(2,1)S(1)}, bf16[4,4,4,16,128]{4,3,2,1,0:T(8,128)(2,1)S(1)}, u32[]{:S(2)}, u32[]{:S(2)}) collective-permute-start(bf16[4,4,4,16,128]{4,3,2,1,0:T(8,128)(2,1)S(1)} %get-tuple-element.28), channel_id=1, source_target_pairs={{0,12},{4,8},{8,4},{12,0},{16,28},{20,24},{24,20},{28,16},{1,13},{... | collective-permute-start | bytes 786440 | tf_op jit(solution)/shard_map/ppermute | solution.py:307
  31.7 12.0 %collective-permute-start.6 = (bf16[4,4,4,16,128]{4,3,2,1,0:T(8,128)(2,1)S(1)}, bf16[4,4,4,16,128]{4,3,2,1,0:T(8,128)(2,1)S(1)}, u32[]{:S(2)}, u32[]{:S(2)}) collective-permute-start(bf16[4,4,4,16,128]{4,3,2,1,0:T(8,128)(2,1)S(1)} %get-tuple-element.29), channel_id=1, source_target_pairs={{0,16},{4,20},{8,24},{12,28},{16,0},{20,4},{24,8},{28,12},{1,17},{... | collective-permute-start | bytes 786440 | tf_op jit(solution)/shard_map/ppermute | solution.py:307
  33.3 23.3 %collective-permute-start.7 = (bf16[4,4,4,16,128]{4,3,2,1,0:T(8,128)(2,1)S(1)}, bf16[4,4,4,16,128]{4,3,2,1,0:T(8,128)(2,1)S(1)}, u32[]{:S(2)}, u32[]{:S(2)}) collective-permute-start(bf16[4,4,4,16,128]{4,3,2,1,0:T(8,128)(2,1)S(1)} %get-tuple-element.30), channel_id=1, source_target_pairs={{0,20},{4,16},{8,28},{12,24},{16,4},{20,0},{24,12},{28,8},{1,21},{... | collective-permute-start | bytes 786440 | tf_op jit(solution)/shard_map/ppermute | solution.py:307
  33.4 23.1 %collective-permute-start.8 = (bf16[4,4,4,16,128]{4,3,2,1,0:T(8,128)(2,1)S(1)}, bf16[4,4,4,16,128]{4,3,2,1,0:T(8,128)(2,1)S(1)}, u32[]{:S(2)}, u32[]{:S(2)}) collective-permute-start(bf16[4,4,4,16,128]{4,3,2,1,0:T(8,128)(2,1)S(1)} %get-tuple-element.31), channel_id=1, source_target_pairs={{0,24},{4,28},{8,16},{12,20},{16,8},{20,12},{24,0},{28,4},{1,25},{... | collective-permute-start | bytes 786440 | tf_op jit(solution)/shard_map/ppermute | solution.py:307
  39.1 17.5 %collective-permute-start.9 = (bf16[4,4,4,16,128]{4,3,2,1,0:T(8,128)(2,1)S(1)}, bf16[4,4,4,16,128]{4,3,2,1,0:T(8,128)(2,1)}, u32[]{:S(2)}, u32[]{:S(2)}) collective-permute-start(bf16[4,4,4,16,128]{4,3,2,1,0:T(8,128)(2,1)S(1)} %get-tuple-element.32), channel_id=1, source_target_pairs={{0,28},{4,24},{8,20},{12,16},{16,12},{20,8},{24,4},{28,0},{1,29},{... | collective-permute-start | bytes 786440 | tf_op jit(solution)/shard_map/ppermute | solution.py:307
  41.1 0.7 copy-start.7
  56.6 1.2 copy-start.1
  57.8 0.7 copy-start.5
  90.1 13.2 %collective-permute-start.10 = (bf16[4,4,4,16,128]{4,3,2,1,0:T(8,128)(2,1)S(1)}, bf16[4,4,4,16,128]{4,3,2,1,0:T(8,128)(2,1)S(1)}, u32[]{:S(2)}, u32[]{:S(2)}) collective-permute-start(bf16[4,4,4,16,128]{4,3,2,1,0:T(8,128)(2,1)S(1)} %get-tuple-element.34), channel_id=1, source_target_pairs={{0,4},{4,0},{8,12},{12,8},{16,20},{20,16},{24,28},{28,24},{1,5},{5... | collective-permute-start | bytes 786440 | tf_op jit(solution)/shard_map/ppermute | solution.py:307
  90.2 18.1 %collective-permute-start.11 = (bf16[4,4,4,16,128]{4,3,2,1,0:T(8,128)(2,1)S(1)}, bf16[4,4,4,16,128]{4,3,2,1,0:T(8,128)(2,1)S(1)}, u32[]{:S(2)}, u32[]{:S(2)}) collective-permute-start(bf16[4,4,4,16,128]{4,3,2,1,0:T(8,128)(2,1)S(1)} %get-tuple-element.35), channel_id=1, source_target_pairs={{0,8},{4,12},{8,0},{12,4},{16,24},{20,28},{24,16},{28,20},{1,9},{5... | collective-permute-start | bytes 786440 | tf_op jit(solution)/shard_map/ppermute | solution.py:307
  101.2 12.3 %collective-permute-start.12 = (bf16[4,4,4,16,128]{4,3,2,1,0:T(8,128)(2,1)S(1)}, bf16[4,4,4,16,128]{4,3,2,1,0:T(8,128)(2,1)S(1)}, u32[]{:S(2)}, u32[]{:S(2)}) collective-permute-start(bf16[4,4,4,16,128]{4,3,2,1,0:T(8,128)(2,1)S(1)} %get-tuple-element.36), channel_id=1, source_target_pairs={{0,12},{4,8},{8,4},{12,0},{16,28},{20,24},{24,20},{28,16},{1,13},{... | collective-permute-start | bytes 786440 | tf_op jit(solution)/shard_map/ppermute | solution.py:307
  101.3 12.2 %collective-permute-start.13 = (bf16[4,4,4,16,128]{4,3,2,1,0:T(8,128)(2,1)S(1)}, bf16[4,4,4,16,128]{4,3,2,1,0:T(8,128)(2,1)S(1)}, u32[]{:S(2)}, u32[]{:S(2)}) collective-permute-start(bf16[4,4,4,16,128]{4,3,2,1,0:T(8,128)(2,1)S(1)} %get-tuple-element.37), channel_id=1, source_target_pairs={{0,16},{4,20},{8,24},{12,28},{16,0},{20,4},{24,8},{28,12},{1,17},{... | collective-permute-start | bytes 786440 | tf_op jit(solution)/shard_map/ppermute | solution.py:307
  103.0 23.7 %collective-permute-start.14 = (bf16[4,4,4,16,128]{4,3,2,1,0:T(8,128)(2,1)S(1)}, bf16[4,4,4,16,128]{4,3,2,1,0:T(8,128)(2,1)S(1)}, u32[]{:S(2)}, u32[]{:S(2)}) collective-permute-start(bf16[4,4,4,16,128]{4,3,2,1,0:T(8,128)(2,1)S(1)} %get-tuple-element.38), channel_id=1, source_target_pairs={{0,20},{4,16},{8,28},{12,24},{16,4},{20,0},{24,12},{28,8},{1,21},{... | collective-permute-start | bytes 786440 | tf_op jit(solution)/shard_map/ppermute | solution.py:307
  103.4 23.4 %collective-permute-start.15 = (bf16[4,4,4,16,128]{4,3,2,1,0:T(8,128)(2,1)S(1)}, bf16[4,4,4,16,128]{4,3,2,1,0:T(8,128)(2,1)S(1)}, u32[]{:S(2)}, u32[]{:S(2)}) collective-permute-start(bf16[4,4,4,16,128]{4,3,2,1,0:T(8,128)(2,1)S(1)} %get-tuple-element.39), channel_id=1, source_target_pairs={{0,24},{4,28},{8,16},{12,20},{16,8},{20,12},{24,0},{28,4},{1,25},{... | collective-permute-start | bytes 786440 | tf_op jit(solution)/shard_map/ppermute | solution.py:307
  108.4 18.4 %collective-permute-start.16 = (bf16[4,4,4,16,128]{4,3,2,1,0:T(8,128)(2,1)S(1)}, bf16[4,4,4,16,128]{4,3,2,1,0:T(8,128)(2,1)S(1)}, u32[]{:S(2)}, u32[]{:S(2)}) collective-permute-start(bf16[4,4,4,16,128]{4,3,2,1,0:T(8,128)(2,1)S(1)} %get-tuple-element.40), channel_id=1, source_target_pairs={{0,28},{4,24},{8,20},{12,16},{16,12},{20,8},{24,4},{28,0},{1,29},{... | collective-permute-start | bytes 786440 | tf_op jit(solution)/shard_map/ppermute | solution.py:307
  128.0 11.8 %collective-permute-start.17 = (bf16[16,4,16,128]{3,2,1,0:T(8,128)(2,1)S(1)}, bf16[16,4,16,128]{3,2,1,0:T(8,128)(2,1)S(1)}, u32[]{:S(2)}, u32[]{:S(2)}) collective-permute-start(bf16[16,4,16,128]{3,2,1,0:T(8,128)(2,1)S(1)} %get-tuple-element.42), channel_id=1, source_target_pairs={{0,1},{1,0},{2,3},{3,2},{4,5},{5,4},{6,7},{7,6},{8,9},{9,8},{10,11... | collective-permute-start | bytes 786440 | tf_op jit(solution)/shard_map/ppermute | solution.py:307
  128.1 21.4 %collective-permute-start.18 = (bf16[16,4,16,128]{3,2,1,0:T(8,128)(2,1)S(1)}, bf16[16,4,16,128]{3,2,1,0:T(8,128)(2,1)S(1)}, u32[]{:S(2)}, u32[]{:S(2)}) collective-permute-start(bf16[16,4,16,128]{3,2,1,0:T(8,128)(2,1)S(1)} %get-tuple-element.43), channel_id=1, source_target_pairs={{0,2},{1,3},{2,0},{3,1},{4,6},{5,7},{6,4},{7,5},{8,10},{9,11},{10,... | collective-permute-start | bytes 786440 | tf_op jit(solution)/shard_map/ppermute | solution.py:307
  128.1 21.3 %collective-permute-start.19 = (bf16[16,4,16,128]{3,2,1,0:T(8,128)(2,1)S(1)}, bf16[16,4,16,128]{3,2,1,0:T(8,128)(2,1)S(1)}, u32[]{:S(2)}, u32[]{:S(2)}) collective-permute-start(bf16[16,4,16,128]{3,2,1,0:T(8,128)(2,1)S(1)} %get-tuple-element.44), channel_id=1, source_target_pairs={{0,3},{1,2},{2,1},{3,0},{4,7},{5,6},{6,5},{7,4},{8,11},{9,10},{10,... | collective-permute-start | bytes 786440 | tf_op jit(solution)/shard_map/ppermute | solution.py:307

commit v2 on v1

--- a/solution.py
+++ b/solution.py
@@ -14,6 +14,7 @@
 SCREENING = 0.02
 F32 = jnp.float32
 BF16 = jnp.bfloat16
+CHOOSE_HINT = 60 * 10**9
 VMEM_BYTES = 44 * 1024 * 1024
 
 
@@ -103,39 +104,37 @@
             out[2 * xh + 1, :, j * wide : (j + 1) * wide] = second
 
 
-def choose_kernel(pair_total, grid_total, capacity, place, boxes, *refs):
-    parts, outs = refs[:pair_total], refs[pair_total:]
-    me, mate = place[0], place[1]
-    for turn, out in enumerate(outs):
-        target = lax.bitwise_xor(me, turn)
+def choose_kernel(pair_total, capacity, place, boxes, *refs):
+    parts, outs = refs[:-1], refs[-1]
+    mate = place[1]
+    for target in range(outs.shape[0]):
         for slot in range(capacity):
             orbital = boxes[(target * pair_total + mate) * capacity + slot]
             for step, part in enumerate(parts):
-                out[slot, :, lax.bitwise_xor(mate, step)] = part[orbital]
-
-
-def gather_kernel(pair_total, grid_total, capacity, place, boxes, *refs):
-    parts, outs, total = refs[:grid_total], refs[grid_total:-1], refs[-1]
-    me, mate = place[0], place[1]
+                outs[target, slot, :, step] = part[orbital]
+
+
+def gather_kernel(pair_total, capacity, place, boxes, landed, *refs):
+    outs, total = refs[:-1], refs[-1]
+    mate = place[1]
     total[...] = jnp.zeros_like(total)
-    for turn, part in enumerate(parts):
-        origin = lax.bitwise_xor(me, turn)
+    for origin in range(landed.shape[0]):
         for slot in range(capacity):
             orbital = boxes[(origin * pair_total + mate) * capacity + slot]
-            total[orbital] += part[slot].astype(F32)
+            total[orbital] += landed[origin, slot].astype(F32)
     for step, out in enumerate(outs):
-        out[...] = total[:, :, lax.bitwise_xor(mate, step)].astype(out.dtype)
-
-
-def worker_kernel(extent, grid_total, place, slots, offsets, count, *refs):
-    parts = refs[:grid_total]
-    table_y, ahead, back, table_z, green = refs[grid_total : grid_total + 5]
-    outs = refs[grid_total + 5 : 2 * grid_total + 5]
-    box, shifted, first, second, returned, collected = refs[2 * grid_total + 5 :]
-    capacity, local, pair_total, heights, wide = parts[0].shape
+        out[...] = total[:, :, step].astype(out.dtype)
+
+
+def worker_kernel(extent, place, slots, offsets, count, *refs):
+    parts = refs[:2]
+    table_y, ahead, back, table_z, green = refs[2:7]
+    outs = refs[7:9]
+    box, shifted, first, second, returned, collected = refs[9:]
+    grid_total, capacity, local, _, heights, wide = parts[0].shape
+    mate = place[1]
     half = extent // 2
     edge = SHIFT // 2
-    me = place[0]
     low = lane_low(extent)
     lanes = lax.broadcasted_iota(jnp.int32, (1, wide), 1)
     depth = lanes - jnp.where(low, 0, extent)
@@ -153,14 +152,22 @@
     clear(returned)
     for slot in range(capacity):
         clear(box.at[slot])
-    for turn, part in enumerate(parts):
-        start = edge + lax.bitwise_xor(me, turn) * local
-        for slot in range(capacity):
-            for xh in range(local):
-                for p in range(pair_total):
-                    box[slot, start + xh, SHIFT + p * heights : SHIFT + (p + 1) * heights] = part[
-                        slot, xh, p
-                    ].astype(F32)
+    def all_rows(visit):
+        step = 0
+        for chunk, part in enumerate(parts):
+            for index in range(part.shape[3]):
+                row = lax.bitwise_xor(mate, step) * heights
+                step += 1
+                for origin in range(grid_total):
+                    for slot in range(capacity):
+                        for xh in range(local):
+                            visit(chunk, (origin, slot, xh, index), slot, origin * local + xh, row)
+
+    def fill(chunk, index, slot, xh, row):
+        rows = pl.ds(pl.multiple_of(SHIFT + row, 8), heights)
+        box[slot, edge + xh, rows] = parts[chunk][index].astype(F32)
+
+    all_rows(fill)
 
     def moved(ref, xh, steps):
         step_x, step_y, step_z = steps
@@ -181,25 +188,25 @@
         opposite = tuple(-s for s in steps)
 
         def load_y(group, carry):
-            for pair in range(2):
+            for pair in range(16):
                 stacks = []
                 for member in range(2):
-                    xh = group * 4 + pair * 2 + member
+                    xh = group * 32 + pair * 2 + member
                     other = moved(box.at[slot_b], xh, steps)
                     shifted[xh] = other
                     own = box[slot_a, edge + xh, SHIFT : SHIFT + extent]
                     stacks.append(three(own * other, 0))
                 done = mul(table_y[...], jnp.concatenate(stacks, axis=1))
                 for member in range(2):
-                    xh = group * 4 + pair * 2 + member
+                    xh = group * 32 + pair * 2 + member
                     first[pl.ds(pl.multiple_of(xh * extent, extent), extent), :] = done[
                         :, member * wide : (member + 1) * wide
                     ]
             return carry
 
-        lax.fori_loop(0, half // 4, load_y, 0)
-
-        many = 8
+        lax.fori_loop(0, half // 32, load_y, 0)
+
+        many = 64
 
         def middle(group, carry):
             def apply_x(table, values):
@@ -227,15 +234,15 @@
         lax.fori_loop(0, extent // many, middle, 0)
 
         def unload_y(group, carry):
-            for pair in range(2):
+            for pair in range(16):
                 stacks = []
                 for member in range(2):
-                    xh = group * 4 + pair * 2 + member
+                    xh = group * 32 + pair * 2 + member
                     rows = pl.ds(pl.multiple_of(xh * extent, extent), extent)
                     stacks.append(three(second[rows, :], 0))
                 done = mul(table_y[...], jnp.concatenate(stacks, axis=1))
                 for member in range(2):
-                    xh = group * 4 + pair * 2 + member
+                    xh = group * 32 + pair * 2 + member
                     potential = done[:, member * wide : (member + 1) * wide]
                     value = potential * shifted[xh]
                     if fresh:
@@ -246,11 +253,11 @@
                     returned[edge + xh, SHIFT : SHIFT + extent] = potential * own
             return carry
 
-        lax.fori_loop(0, half // 4, unload_y, 0)
+        lax.fori_loop(0, half // 32, unload_y, 0)
 
         def give(group, carry):
-            for member in range(4):
-                xh = group * 4 + member
+            for member in range(32):
+                xh = group * 32 + member
                 value = moved(returned, xh, opposite)
                 if fresh:
                     collected[slot_b, xh] = value
@@ -258,7 +265,7 @@
                     collected[slot_b, xh] += value
             return carry
 
-        lax.fori_loop(0, half // 4, give, 0)
+        lax.fori_loop(0, half // 32, give, 0)
 
     def opening(turn, carry):
         one_pair(turn, True)
@@ -271,14 +278,11 @@
     lax.fori_loop(0, capacity // 2, opening, 0)
     lax.fori_loop(capacity // 2, count[0], later, 0)
 
-    for turn, out in enumerate(outs):
-        start = lax.bitwise_xor(me, turn) * local
-        for slot in range(capacity):
-            for xh in range(local):
-                for p in range(pair_total):
-                    out[slot, xh, p] = collected[
-                        slot, start + xh, p * heights : (p + 1) * heights
-                    ].astype(BF16)
+    def empty(chunk, index, slot, xh, row):
+        rows = pl.ds(pl.multiple_of(row, 8), heights)
+        outs[chunk][index] = collected[slot, xh, rows].astype(BF16)
+
+    all_rows(empty)
 
 
 def spec(count):
@@ -302,50 +306,15 @@
     )(*inputs)
 
 
-def swap(arrays, axis, total):
-    return [
-        array if k == 0 else lax.ppermute(array, axis, [(i, i ^ k) for i in range(total)])
-        for k, array in enumerate(arrays)
-    ]
-
-
-def shards(grid_total, pair_total, orbitals, box_list, pair_slots, offsets, pair_count):
-    planes, orbital_total, cells = orbitals.shape
-    capacity = box_list.shape[2]
-    extent = planes * grid_total
-    heights = cells // extent
-    local, half, wide = planes // 2, extent // 2, 2 * extent
+def worker_call(extent, place, slots, offsets, count, arrived, constants):
+    capacity = arrived[0].shape[1]
+    half, wide = extent // 2, 2 * extent
     padded_x, padded_y = half + SHIFT + 1, extent + 2 * SHIFT
-    place = jnp.stack([lax.axis_index("grid"), lax.axis_index("pair")]).astype(jnp.int32)
-    boxes = box_list.reshape(-1)
-    shape = jax.ShapeDtypeStruct
-
-    piece = (orbital_total, local, heights, wide)
-    rows = pltpu.VMEM((math.prod(piece[:-1]), wide), F32)
-    bundle = (capacity, local, pair_total, heights, wide)
-
-    (own,) = call(functools.partial(pieces_kernel, extent), 0, [orbitals], [shape(piece, BF16)], [rows])
-    gathered = swap([own] * pair_total, "pair", pair_total)
-    outgoing = call(
-        functools.partial(choose_kernel, pair_total, grid_total, capacity),
-        2,
-        [place, boxes, *gathered],
-        [shape(bundle, BF16)] * grid_total,
-        [],
-    )
-    arrived = swap(outgoing, "grid", grid_total)
-    fields = call(
-        functools.partial(worker_kernel, extent, grid_total),
+    return call(
+        functools.partial(worker_kernel, extent),
         4,
-        [
-            place,
-            pair_slots.reshape(-1),
-            offsets.reshape(-1),
-            pair_count.reshape(-1),
-            *arrived,
-            *(jnp.asarray(t) for t in tables(extent)),
-        ],
-        [shape(bundle, BF16)] * grid_total,
+        [place, slots, offsets, count, *arrived, *constants],
+        [jax.ShapeDtypeStruct(a.shape, BF16) for a in arrived],
         [
             pltpu.VMEM((capacity, padded_x, padded_y, wide), F32),
             pltpu.VMEM((half, extent, wide), F32),
@@ -356,15 +325,64 @@
         ],
         flops=3 * 2 * 6 * 3 * extent**4,
     )
-    landed = swap(fields, "grid", grid_total)
-    sums = call(
-        functools.partial(gather_kernel, pair_total, grid_total, capacity),
-        2,
-        [place, boxes, *landed],
-        [shape(piece, F32)] + [shape(piece, BF16)] * (pair_total - 1),
-        [pltpu.VMEM((orbital_total, local, pair_total, heights, wide), F32)],
+
+
+def over_pair(array, step, total):
+    return array if step == 0 else lax.ppermute(array, "pair", [(i, i ^ step) for i in range(total)])
+
+
+def over_grid(array):
+    return lax.all_to_all(array, "grid", 0, 0, tiled=True)
+
+
+def shards(grid_total, pair_total, orbitals, box_list, pair_slots, offsets, pair_count):
+    planes, orbital_total, cells = orbitals.shape
+    capacity = box_list.shape[2]
+    extent = planes * grid_total
+    heights = cells // extent
+    local, wide = planes // 2, 2 * extent
+    place = jnp.stack([lax.axis_index("grid"), lax.axis_index("pair")]).astype(jnp.int32)
+    boxes = box_list.reshape(-1)
+    shape = jax.ShapeDtypeStruct
+    chunks = (range(pair_total // 2), range(pair_total // 2, pair_total))
+
+    piece = (orbital_total, local, heights, wide)
+    rows = pltpu.VMEM((math.prod(piece[:-1]), wide), F32)
+
+    (own,) = call(functools.partial(pieces_kernel, extent), 0, [orbitals], [shape(piece, BF16)], [rows])
+    gathered = [over_pair(own, step, pair_total) for step in range(pair_total)]
+    arrived = []
+    for chunk in chunks:
+        bundle = (grid_total, capacity, local, len(chunk), heights, wide)
+        (outgoing,) = call(
+            functools.partial(choose_kernel, pair_total, capacity),
+            2,
+            [place, boxes, *(gathered[step] for step in chunk)],
+            [shape(bundle, BF16)],
+            [],
+            flops=CHOOSE_HINT,
+        )
+        arrived.append(over_grid(outgoing))
+    fields = worker_call(
+        extent,
+        place,
+        pair_slots.reshape(-1),
+        offsets.reshape(-1),
+        pair_count.reshape(-1),
+        arrived,
+        [jnp.asarray(t) for t in tables(extent)],
     )
-    parts = swap(sums, "pair", pair_total)
+    parts = [None] * pair_total
+    for chunk, field in reversed(list(zip(chunks, fields))):
+        sums = call(
+            functools.partial(gather_kernel, pair_total, capacity),
+            2,
+            [place, boxes, over_grid(field)],
+            [shape(piece, F32 if step == 0 else BF16) for step in chunk],
+            [pltpu.VMEM((orbital_total, local, len(chunk), heights, wide), F32)],
+        )
+        for step, value in zip(chunk, sums):
+            parts[step] = over_pair(value, step, pair_total)
     (result,) = call(
         functools.partial(slab_kernel, extent), 0, parts, [shape(orbitals.shape, F32)], [rows]
     )

time: 154 us -> 120 us (0.78); the launches traced: 151 us -> 120 us
  waiting for transfers between devices: 75.4 us -> 47.7 us
  blocking collectives: 0 us -> 17.8 us
  Pallas kernels: 35.5 us -> 25.7 us
  starting transfers between devices: 35 us -> 25.7 us
  local copies, waits for them, and re-layouts: 4.08 us -> 2.16 us
    ppermute x20 -> x6, waiting for transfers between devices: 75.4 us -> 26.7 us  [over_pair(): lax.ppermute(array, 'pair', [(i, i ^ step) for i in range(total)])]
    all_to_all x0 -> x3, waiting for transfers between devices: none -> 21 us  [over_grid(): return lax.all_to_all(array, 'grid', 0, 0, tiled=True)]
    ppermute x20 -> x6, starting transfers between devices: 35 us -> 14.9 us  [over_pair(): lax.ppermute(array, 'pair', [(i, i ^ step) for i in range(total)])]
    all_to_all x0 -> x1, blocking collectives: none -> 17.8 us  [over_grid(): return lax.all_to_all(array, 'grid', 0, 0, tiled=True)]
    all_to_all x0 -> x3, starting transfers between devices: none -> 10.8 us  [over_grid(): return lax.all_to_all(array, 'grid', 0, 0, tiled=True)]
    pallas_call x5 -> x7, Pallas kernels: 35.5 us -> 25.7 us  [call(): pl.pallas_call(kernel, out_shape=out_shapes, in_specs=scalars(scalar_coun...]
    unnamed x21, local copies, waits for them, and re-layouts: 3.8 us -> 1.88 us
  transfers between devices with their start and end apart: 20 -> 9, of which waited for: 10 -> 8; matrix products, arithmetic and copies ran while one was open for 0% -> 1% of each run, Pallas kernels for 0% -> 4%
where the time goes in v2:
time: 120 us
  waiting for transfers between devices  47.7 us (40%)
  Pallas kernels  25.7 us (21%)
  starting transfers between devices  25.7 us (21%)
  blocking collectives  17.8 us (15%)
  local copies, waits for them, and re-layouts  2.16 us (2%)
    ppermute x6, waiting for transfers between devices, over_pair(): lax.ppermute(array, 'pair', [(i, i ^ step) for i in range(total)])  26.7 us
    pallas_call x7, Pallas kernels, call(): pl.pallas_call(kernel, out_shape=out_shapes, in_specs=scalars(scalar_coun...  25.7 us
    all_to_all x3, waiting for transfers between devices, over_grid(): return lax.all_to_all(array, 'grid', 0, 0, tiled=True)  21 us
    all_to_all x1, blocking collectives, over_grid(): return lax.all_to_all(array, 'grid', 0, 0, tiled=True)  17.8 us
    ppermute x6, starting transfers between devices, over_pair(): lax.ppermute(array, 'pair', [(i, i ^ step) for i in range(total)])  14.9 us
    all_to_all x3, starting transfers between devices, over_grid(): return lax.all_to_all(array, 'grid', 0, 0, tiled=True)  10.8 us
  transfers between devices with their start and end apart: 9, of which 8 were waited for; matrix products, arithmetic and copies ran while one was open for 1% of the time, Pallas kernels for 4%

profile of v2, /device:TPU:0, one launch (start us, length us, event | category | flops | bytes accessed | tf_op | source)
XLA Modules:
  0.0 119.8 jit_solution(12878262394959180527)
XLA Ops:
  0.0 0.0 copy-start
  0.0 0.9 copy-done
  1.0 0.5 shard_map.100.refs_0_
  1.5 0.0 copy-start.6
  1.5 3.1 %collective-permute-start = (bf16[16,4,16,128]{3,2,1,0:T(8,128)(2,1)S(1)}, bf16[16,4,16,128]{3,2,1,0:T(8,128)(2,1)S(1)}, u32[]{:S(2)}, u32[]{:S(2)}) collective-permute-start(bf16[16,4,16,128]{3,2,1,0:T(8,128)(2,1)S(1)} %shard_map.100.refs_0_), channel_id=1, source_target_pairs={{0,1},{1,0},{2,3},{3,2},{4,5},{5,4},{6,7},{7,6},{8,9},{9,8},{10,11... | collective-permute-start | bytes 786440 | tf_op jit(solution)/shard_map/ppermute | solution.py:331
  4.6 2.5 %collective-permute-start.2 = (bf16[16,4,16,128]{3,2,1,0:T(8,128)(2,1)S(1)}, bf16[16,4,16,128]{3,2,1,0:T(8,128)(2,1)S(1)}, u32[]{:S(2)}, u32[]{:S(2)}) collective-permute-start(bf16[16,4,16,128]{3,2,1,0:T(8,128)(2,1)S(1)} %shard_map.100.refs_0_), channel_id=1, source_target_pairs={{0,3},{1,2},{2,1},{3,0},{4,7},{5,6},{6,5},{7,4},{8,11},{9,10},{10,... | collective-permute-start | bytes 786440 | tf_op jit(solution)/shard_map/ppermute | solution.py:331
  7.0 0.1 collective-permute-start.1
  7.2 0.0 copy-done.6
  7.2 0.1 copy.14
  7.3 0.1 reshape.12.boxes
  7.4 0.1 pad_add_fusion.place
  7.5 3.8 %collective-permute-done.refs_1_ = bf16[16,4,16,128]{3,2,1,0:T(8,128)(2,1)S(1)} collective-permute-done((bf16[16,4,16,128]{3,2,1,0:T(8,128)(2,1)S(1)}, bf16[16,4,16,128]{3,2,1,0:T(8,128)(2,1)S(1)}, u32[]{:S(2)}, u32[]{:S(2)}) %collective-permute-start) | collective-permute-done | bytes 262176 | tf_op jit(solution)/shard_map/ppermute | solution.py:331
  11.3 1.6 %shard_map.101 = bf16[8,4,4,2,16,128]{5,4,3,2,1,0:T(8,128)(2,1)} custom-call(s32[2]{0:T(128)S(1)} %pad_add_fusion.place, s32[128]{0:T(128)S(1)} %reshape.12.boxes, bf16[16,4,16,128]{3,2,1,0:T(8,128)(2,1)S(1)} %shard_map.100.refs_0_, bf16[16,4,16,128]{3,2,1,0:T(8,128)(2,1)S(1)} %collective-permute-done.refs_1_), custom_call_target="tpu_custom_call" | custom-call | flops 60000002048 | bytes 1573384 | tf_op jit(solution)/shard_map/pallas_call | solution.py:298
  12.9 3.7 %all-to-all-start = ((bf16[8,4,4,2,16,128]{5,4,3,2,1,0:T(8,128)(2,1)}), bf16[8,4,4,2,16,128]{5,4,3,2,1,0:T(8,128)(2,1)S(1)}, u32[]{:S(2)}, u32[]{:S(2)}) async-start(bf16[8,4,4,2,16,128]{5,4,3,2,1,0:T(8,128)(2,1)} %shard_map.101), calls=%async_computation | async-start | bytes 2097152 | tf_op jit(solution)/shard_map/all_to_all | solution.py:335
  16.6 3.3 %collective-permute-done.2.refs_1_ = bf16[16,4,16,128]{3,2,1,0:T(8,128)(2,1)S(1)} collective-permute-done((bf16[16,4,16,128]{3,2,1,0:T(8,128)(2,1)S(1)}, bf16[16,4,16,128]{3,2,1,0:T(8,128)(2,1)S(1)}, u32[]{:S(2)}, u32[]{:S(2)}) %collective-permute-start.2) | collective-permute-done | bytes 262176 | tf_op jit(solution)/shard_map/ppermute | solution.py:331
  19.9 10.1 %collective-permute-done.1.refs_0_ = bf16[16,4,16,128]{3,2,1,0:T(8,128)(2,1)S(1)} collective-permute-done((bf16[16,4,16,128]{3,2,1,0:T(8,128)(2,1)S(1)}, bf16[16,4,16,128]{3,2,1,0:T(8,128)(2,1)S(1)}, u32[]{:S(2)}, u32[]{:S(2)}) %collective-permute-start.1) | collective-permute-done | bytes 262176 | tf_op jit(solution)/shard_map/ppermute | solution.py:331
  30.0 1.6 %shard_map.102 = bf16[8,4,4,2,16,128]{5,4,3,2,1,0:T(8,128)(2,1)} custom-call(s32[2]{0:T(128)S(1)} %pad_add_fusion.place, s32[128]{0:T(128)S(1)} %reshape.12.boxes, bf16[16,4,16,128]{3,2,1,0:T(8,128)(2,1)S(1)} %collective-permute-done.1.refs_0_, bf16[16,4,16,128]{3,2,1,0:T(8,128)(2,1)S(1)} %collective-permute-done.2.refs_1_), custom_call_target="tpu_custom_call" | custom-call | flops 60000002048 | bytes 1573384 | tf_op jit(solution)/shard_map/pallas_call | solution.py:298
  31.6 0.0 copy-start.1
  31.6 0.0 copy-start.2
  31.6 0.0 copy-start.3
  31.6 0.0 copy-start.4
  31.6 0.0 copy-start.5
  31.6 0.4 all-to-all-done.refs_0_
  32.0 3.6 %all-to-all-start.1 = ((bf16[8,4,4,2,16,128]{5,4,3,2,1,0:T(8,128)(2,1)}), bf16[8,4,4,2,16,128]{5,4,3,2,1,0:T(8,128)(2,1)S(1)}, u32[]{:S(2)}, u32[]{:S(2)}) async-start(bf16[8,4,4,2,16,128]{5,4,3,2,1,0:T(8,128)(2,1)} %shard_map.102), calls=%async_computation.1 | async-start | bytes 2097152 | tf_op jit(solution)/shard_map/all_to_all | solution.py:335
  35.6 0.0 copy-start.8
  36.3 0.0 copy-done.8
  36.3 0.1 copy.15
  36.4 0.0 copy-start.7
  36.4 0.1 reshape.13.slots
  36.5 0.6 copy-done.7
  37.1 0.1 copy.16
  37.1 0.1 reshape.14.offsets
  37.2 13.7 %all-to-all-done.1.refs_1_ = bf16[8,4,4,2,16,128]{5,4,3,2,1,0:T(8,128)(2,1)S(1)} async-done(((bf16[8,4,4,2,16,128]{5,4,3,2,1,0:T(8,128)(2,1)}), bf16[8,4,4,2,16,128]{5,4,3,2,1,0:T(8,128)(2,1)S(1)}, u32[]{:S(2)}, u32[]{:S(2)}) %all-to-all-start.1) | async-done | bytes 1048608 | tf_op jit(solution)/shard_map/all_to_all | solution.py:335
  50.9 0.0 copy-done.1
  50.9 0.0 copy-done.2
  50.9 0.0 copy-done.3
  50.9 0.0 copy-done.4
  51.0 0.0 copy-done.5
  51.0 18.8 %shard_map.103 = (bf16[8,4,4,2,16,128]{5,4,3,2,1,0:T(8,128)(2,1)}, bf16[8,4,4,2,16,128]{5,4,3,2,1,0:T(8,128)(2,1)S(1)}) custom-call(s32[2]{0:T(128)S(1)} %pad_add_fusion.place, s32[8]{0:T(128)S(1)} %reshape.13.slots, s32[12]{0:T(128)S(1)} %reshape.14.offsets, s32[1]{0:T(128)} %bitcast.3.count, bf16[8,4,4,2,16,128]{5,4,3,2,1,0:T(8,128)(2,1)S(1)} %all-to-all-done.refs_0_, ...), custom_call_target="tpu_custom_call" | custom-call | flops 1811939328 | bytes 5390428 | tf_op jit(solution)/shard_map/pallas_call | solution.py:298
  69.8 17.8 %all_to_all.20.landed = bf16[8,4,4,2,16,128]{5,4,3,2,1,0:T(8,128)(2,1)S(1)} all-to-all(bf16[8,4,4,2,16,128]{5,4,3,2,1,0:T(8,128)(2,1)S(1)} %get-tuple-element.14), channel_id=1, replica_groups=mesh['grid'=8,'pair'=4] {'grid'}, dimensions={0} | all-to-all | bytes 2097152 | tf_op jit(solution)/shard_map/all_to_all | solution.py:335
  87.6 3.6 %all-to-all-start.2 = ((bf16[8,4,4,2,16,128]{5,4,3,2,1,0:T(8,128)(2,1)}), bf16[8,4,4,2,16,128]{5,4,3,2,1,0:T(8,128)(2,1)S(1)}, u32[]{:S(2)}, u32[]{:S(2)}) async-start(bf16[8,4,4,2,16,128]{5,4,3,2,1,0:T(8,128)(2,1)} %get-tuple-element.11), calls=%async_computation.2 | async-start | bytes 2097152 | tf_op jit(solution)/shard_map/all_to_all | solution.py:335
  91.1 0.9 shard_map.105
  92.0 2.7 %collective-permute-start.4 = (bf16[16,4,16,128]{3,2,1,0:T(8,128)(2,1)S(1)}, bf16[16,4,16,128]{3,2,1,0:T(8,128)(2,1)S(1)}, u32[]{:S(2)}, u32[]{:S(2)}) collective-permute-start(bf16[16,4,16,128]{3,2,1,0:T(8,128)(2,1)S(1)} %get-tuple-element.15), channel_id=1, source_target_pairs={{0,2},{1,3},{2,0},{3,1},{4,6},{5,7},{6,4},{7,5},{8,10},{9,11},{10,... | collective-permute-start | bytes 786440 | tf_op jit(solution)/shard_map/ppermute | solution.py:331
  94.8 4.8 %collective-permute-start.5 = (bf16[16,4,16,128]{3,2,1,0:T(8,128)(2,1)S(1)}, bf16[16,4,16,128]{3,2,1,0:T(8,128)(2,1)S(1)}, u32[]{:S(2)}, u32[]{:S(2)}) collective-permute-start(bf16[16,4,16,128]{3,2,1,0:T(8,128)(2,1)S(1)} %get-tuple-element.16), channel_id=1, source_target_pairs={{0,3},{1,2},{2,1},{3,0},{4,7},{5,6},{6,5},{7,4},{8,11},{9,10},{10,... | collective-permute-start | bytes 786440 | tf_op jit(solution)/shard_map/ppermute | solution.py:331
  99.6 6.9 %all-to-all-done.2.landed = bf16[8,4,4,2,16,128]{5,4,3,2,1,0:T(8,128)(2,1)S(1)} async-done(((bf16[8,4,4,2,16,128]{5,4,3,2,1,0:T(8,128)(2,1)}), bf16[8,4,4,2,16,128]{5,4,3,2,1,0:T(8,128)(2,1)S(1)}, u32[]{:S(2)}, u32[]{:S(2)}) %all-to-all-start.2) | async-done | bytes 1048608 | tf_op jit(solution)/shard_map/all_to_all | solution.py:335
  106.5 0.9 shard_map.104
  107.4 1.7 %collective-permute-start.3 = (bf16[16,4,16,128]{3,2,1,0:T(8,128)(2,1)S(1)}, bf16[16,4,16,128]{3,2,1,0:T(8,128)(2,1)S(1)}, u32[]{:S(2)}, u32[]{:S(2)}) collective-permute-start(bf16[16,4,16,128]{3,2,1,0:T(8,128)(2,1)S(1)} %get-tuple-element.13), channel_id=1, source_target_pairs={{0,1},{1,0},{2,3},{3,2},{4,5},{5,4},{6,7},{7,6},{8,9},{9,8},{10,11... | collective-permute-start | bytes 786440 | tf_op jit(solution)/shard_map/ppermute | solution.py:331
  109.1 4.3 %collective-permute-done.4.refs_2_ = bf16[16,4,16,128]{3,2,1,0:T(8,128)(2,1)S(1)} collective-permute-done((bf16[16,4,16,128]{3,2,1,0:T(8,128)(2,1)S(1)}, bf16[16,4,16,128]{3,2,1,0:T(8,128)(2,1)S(1)}, u32[]{:S(2)}, u32[]{:S(2)}) %collective-permute-start.4) | collective-permute-done | bytes 262176 | tf_op jit(solution)/shard_map/ppermute | solution.py:331
  113.4 0.0 collective-permute-done.5.refs_3_
  113.4 5.1 %collective-permute-done.3.refs_1_ = bf16[16,4,16,128]{3,2,1,0:T(8,128)(2,1)S(1)} collective-permute-done((bf16[16,4,16,128]{3,2,1,0:T(8,128)(2,1)S(1)}, bf16[16,4,16,128]{3,2,1,0:T(8,128)(2,1)S(1)}, u32[]{:S(2)}, u32[]{:S(2)}) %collective-permute-start.3) | collective-permute-done | bytes 262176 | tf_op jit(solution)/shard_map/ppermute | solution.py:331
  118.5 1.3 %shard_map.106 = f32[8,16,1024]{2,1,0:T(8,128)} custom-call(f32[16,4,16,128]{3,2,1,0:T(8,128)S(1)} %get-tuple-element.12.refs_0_, bf16[16,4,16,128]{3,2,1,0:T(8,128)(2,1)S(1)} %collective-permute-done.3.refs_1_, bf16[16,4,16,128]{3,2,1,0:T(8,128)(2,1)S(1)} %collective-permute-done.4.refs_2_, bf16[16,4,16,128]{3,2,1,0:T(8,128)(2,1)S(1)} %collective-permute-done.5.refs_3_), custom_call_target="tpu_custom_call" | custom-call | bytes 1835008 | tf_op jit(solution)/shard_map/pallas_call | solution.py:298
Async XLA Ops:
  0.0 0.9 copy-start
  1.5 5.7 %copy-start.6 = (s32[8,4,4]{0,2,1:T(4,128)S(1)}, s32[8,4,4]{0,2,1:T(4,128)}, u32[]{:S(2)}) copy-start(s32[8,4,4]{0,2,1:T(4,128)} %param.11) | copy-start | bytes 1540
  1.5 9.8 %collective-permute-start = (bf16[16,4,16,128]{3,2,1,0:T(8,128)(2,1)S(1)}, bf16[16,4,16,128]{3,2,1,0:T(8,128)(2,1)S(1)}, u32[]{:S(2)}, u32[]{:S(2)}) collective-permute-start(bf16[16,4,16,128]{3,2,1,0:T(8,128)(2,1)S(1)} %shard_map.100.refs_0_), channel_id=1, source_target_pairs={{0,1},{1,0},{2,3},{3,2},{4,5},{5,4},{6,7},{7,6},{8,9},{9,8},{10,11... | collective-permute-start | bytes 786440 | tf_op jit(solution)/shard_map/ppermute | solution.py:331
  4.6 15.4 %collective-permute-start.2 = (bf16[16,4,16,128]{3,2,1,0:T(8,128)(2,1)S(1)}, bf16[16,4,16,128]{3,2,1,0:T(8,128)(2,1)S(1)}, u32[]{:S(2)}, u32[]{:S(2)}) collective-permute-start(bf16[16,4,16,128]{3,2,1,0:T(8,128)(2,1)S(1)} %shard_map.100.refs_0_), channel_id=1, source_target_pairs={{0,3},{1,2},{2,1},{3,0},{4,7},{5,6},{6,5},{7,4},{8,11},{9,10},{10,... | collective-permute-start | bytes 786440 | tf_op jit(solution)/shard_map/ppermute | solution.py:331
  7.0 23.0 %collective-permute-start.1 = (bf16[16,4,16,128]{3,2,1,0:T(8,128)(2,1)S(1)}, bf16[16,4,16,128]{3,2,1,0:T(8,128)(2,1)S(1)}, u32[]{:S(2)}, u32[]{:S(2)}) collective-permute-start(bf16[16,4,16,128]{3,2,1,0:T(8,128)(2,1)S(1)} %shard_map.100.refs_0_), channel_id=1, source_target_pairs={{0,2},{1,3},{2,0},{3,1},{4,6},{5,7},{6,4},{7,5},{8,10},{9,11},{10,... | collective-permute-start | bytes 786440 | tf_op jit(solution)/shard_map/ppermute | solution.py:331
  12.9 19.1 %all-to-all-start = ((bf16[8,4,4,2,16,128]{5,4,3,2,1,0:T(8,128)(2,1)}), bf16[8,4,4,2,16,128]{5,4,3,2,1,0:T(8,128)(2,1)S(1)}, u32[]{:S(2)}, u32[]{:S(2)}) async-start(bf16[8,4,4,2,16,128]{5,4,3,2,1,0:T(8,128)(2,1)} %shard_map.101), calls=%async_computation | async-start | bytes 2097152 | tf_op jit(solution)/shard_map/all_to_all | solution.py:335
  31.6 19.3 %copy-start.1 = (f32[64,32,128]{2,1,0:T(8,128)S(1)}, f32[64,32,128]{2,1,0:T(8,128)}, u32[]{:S(2)}) copy-start(f32[64,32,128]{2,1,0:T(8,128)} %constant.23.clone.refs_6_) | copy-start | bytes 3145732
  31.6 19.3 %copy-start.2 = (bf16[384,128]{1,0:T(8,128)(2,1)S(1)}, bf16[384,128]{1,0:T(8,128)(2,1)}, u32[]{:S(2)}) copy-start(bf16[384,128]{1,0:T(8,128)(2,1)} %constant.22.clone.refs_5_) | copy-start | bytes 294916
  31.6 19.3 %copy-start.3 = (bf16[64,192]{1,0:T(8,128)(2,1)S(1)}, bf16[64,192]{1,0:T(8,128)(2,1)}, u32[]{:S(2)}) copy-start(bf16[64,192]{1,0:T(8,128)(2,1)} %constant.19.clone.refs_2_) | copy-start | bytes 73732
  31.6 19.3 %copy-start.4 = (bf16[64,96]{1,0:T(8,128)(2,1)S(1)}, bf16[64,96]{1,0:T(8,128)(2,1)}, u32[]{:S(2)}) copy-start(bf16[64,96]{1,0:T(8,128)(2,1)} %constant.21.clone.refs_4_) | copy-start | bytes 36868
  31.6 19.3 %copy-start.5 = (bf16[64,96]{1,0:T(8,128)(2,1)S(1)}, bf16[64,96]{1,0:T(8,128)(2,1)}, u32[]{:S(2)}) copy-start(bf16[64,96]{1,0:T(8,128)(2,1)} %constant.20.clone.refs_3_) | copy-start | bytes 36868
  32.0 18.9 %all-to-all-start.1 = ((bf16[8,4,4,2,16,128]{5,4,3,2,1,0:T(8,128)(2,1)}), bf16[8,4,4,2,16,128]{5,4,3,2,1,0:T(8,128)(2,1)S(1)}, u32[]{:S(2)}, u32[]{:S(2)}) async-start(bf16[8,4,4,2,16,128]{5,4,3,2,1,0:T(8,128)(2,1)} %shard_map.102), calls=%async_computation.1 | async-start | bytes 2097152 | tf_op jit(solution)/shard_map/all_to_all | solution.py:335
  35.6 0.7 copy-start.8
  36.4 0.7 copy-start.7
  87.6 18.9 %all-to-all-start.2 = ((bf16[8,4,4,2,16,128]{5,4,3,2,1,0:T(8,128)(2,1)}), bf16[8,4,4,2,16,128]{5,4,3,2,1,0:T(8,128)(2,1)S(1)}, u32[]{:S(2)}, u32[]{:S(2)}) async-start(bf16[8,4,4,2,16,128]{5,4,3,2,1,0:T(8,128)(2,1)} %get-tuple-element.11), calls=%async_computation.2 | async-start | bytes 2097152 | tf_op jit(solution)/shard_map/all_to_all | solution.py:335
  92.0 21.4 %collective-permute-start.4 = (bf16[16,4,16,128]{3,2,1,0:T(8,128)(2,1)S(1)}, bf16[16,4,16,128]{3,2,1,0:T(8,128)(2,1)S(1)}, u32[]{:S(2)}, u32[]{:S(2)}) collective-permute-start(bf16[16,4,16,128]{3,2,1,0:T(8,128)(2,1)S(1)} %get-tuple-element.15), channel_id=1, source_target_pairs={{0,2},{1,3},{2,0},{3,1},{4,6},{5,7},{6,4},{7,5},{8,10},{9,11},{10,... | collective-permute-start | bytes 786440 | tf_op jit(solution)/shard_map/ppermute | solution.py:331
  94.8 18.6 %collective-permute-start.5 = (bf16[16,4,16,128]{3,2,1,0:T(8,128)(2,1)S(1)}, bf16[16,4,16,128]{3,2,1,0:T(8,128)(2,1)S(1)}, u32[]{:S(2)}, u32[]{:S(2)}) collective-permute-start(bf16[16,4,16,128]{3,2,1,0:T(8,128)(2,1)S(1)} %get-tuple-element.16), channel_id=1, source_target_pairs={{0,3},{1,2},{2,1},{3,0},{4,7},{5,6},{6,5},{7,4},{8,11},{9,10},{10,... | collective-permute-start | bytes 786440 | tf_op jit(solution)/shard_map/ppermute | solution.py:331
  107.4 11.1 %collective-permute-start.3 = (bf16[16,4,16,128]{3,2,1,0:T(8,128)(2,1)S(1)}, bf16[16,4,16,128]{3,2,1,0:T(8,128)(2,1)S(1)}, u32[]{:S(2)}, u32[]{:S(2)}) collective-permute-start(bf16[16,4,16,128]{3,2,1,0:T(8,128)(2,1)S(1)} %get-tuple-element.13), channel_id=1, source_target_pairs={{0,1},{1,0},{2,3},{3,2},{4,5},{5,4},{6,7},{7,6},{8,9},{9,8},{10,11... | collective-permute-start | bytes 786440 | tf_op jit(solution)/shard_map/ppermute | solution.py:331

commit v3 on v2

--- a/solution.py
+++ b/solution.py
@@ -14,7 +14,9 @@
 SCREENING = 0.02
 F32 = jnp.float32
 BF16 = jnp.bfloat16
-CHOOSE_HINT = 60 * 10**9
+CHOOSE_HINT = (60 * 10**9, 60 * 10**9)
+SPLIT_IN = (False, True)
+SPLIT_OUT = (False, True)
 VMEM_BYTES = 44 * 1024 * 1024
 
 
@@ -104,35 +106,40 @@
             out[2 * xh + 1, :, j * wide : (j + 1) * wide] = second
 
 
-def choose_kernel(pair_total, capacity, place, boxes, *refs):
-    parts, outs = refs[:-1], refs[-1]
-    mate = place[1]
-    for target in range(outs.shape[0]):
+def partners(refs, me):
+    if len(refs) == 1:
+        return [(index, refs[0].at[index]) for index in range(refs[0].shape[0])]
+    return [(lax.bitwise_xor(me, turn), ref) for turn, ref in enumerate(refs)]
+
+
+def choose_kernel(pair_total, capacity, part_total, place, boxes, *refs):
+    parts, outs = refs[:part_total], refs[part_total:]
+    for target, out in partners(outs, place[0]):
         for slot in range(capacity):
-            orbital = boxes[(target * pair_total + mate) * capacity + slot]
+            orbital = boxes[(target * pair_total + place[1]) * capacity + slot]
             for step, part in enumerate(parts):
-                outs[target, slot, :, step] = part[orbital]
-
-
-def gather_kernel(pair_total, capacity, place, boxes, landed, *refs):
-    outs, total = refs[:-1], refs[-1]
-    mate = place[1]
+                out[slot, :, step] = part[orbital]
+
+
+def gather_kernel(pair_total, capacity, landed_total, place, boxes, *refs):
+    landed, outs, total = refs[:landed_total], refs[landed_total:-1], refs[-1]
     total[...] = jnp.zeros_like(total)
-    for origin in range(landed.shape[0]):
+    for origin, bundle in partners(landed, place[0]):
         for slot in range(capacity):
-            orbital = boxes[(origin * pair_total + mate) * capacity + slot]
-            total[orbital] += landed[origin, slot].astype(F32)
+            orbital = boxes[(origin * pair_total + place[1]) * capacity + slot]
+            total[orbital] += bundle[slot].astype(F32)
     for step, out in enumerate(outs):
         out[...] = total[:, :, step].astype(out.dtype)
 
 
-def worker_kernel(extent, place, slots, offsets, count, *refs):
-    parts = refs[:2]
-    table_y, ahead, back, table_z, green = refs[2:7]
-    outs = refs[7:9]
-    box, shifted, first, second, returned, collected = refs[9:]
-    grid_total, capacity, local, _, heights, wide = parts[0].shape
-    mate = place[1]
+def worker_kernel(extent, arrived_totals, sent_totals, place, slots, offsets, count, *refs):
+    refs = list(refs)
+    parts = [[refs.pop(0) for _ in range(total)] for total in arrived_totals]
+    table_y, ahead, back, table_z, green = [refs.pop(0) for _ in range(5)]
+    outs = [[refs.pop(0) for _ in range(total)] for total in sent_totals]
+    box, shifted, first, second, returned, collected = refs
+    capacity, local, _, heights, wide = parts[0][-1].shape[-5:]
+    me, mate = place[0], place[1]
     half = extent // 2
     edge = SHIFT // 2
     low = lane_low(extent)
@@ -152,22 +159,22 @@
     clear(returned)
     for slot in range(capacity):
         clear(box.at[slot])
-    def all_rows(visit):
+    def all_rows(lists, visit):
         step = 0
-        for chunk, part in enumerate(parts):
-            for index in range(part.shape[3]):
+        for bundles in lists:
+            for index in range(bundles[0].shape[-3]):
                 row = lax.bitwise_xor(mate, step) * heights
                 step += 1
-                for origin in range(grid_total):
+                for origin, bundle in partners(bundles, me):
                     for slot in range(capacity):
                         for xh in range(local):
-                            visit(chunk, (origin, slot, xh, index), slot, origin * local + xh, row)
-
-    def fill(chunk, index, slot, xh, row):
+                            visit(bundle, (slot, xh, index), origin * local + xh, row)
+
+    def fill(bundle, index, xh, row):
         rows = pl.ds(pl.multiple_of(SHIFT + row, 8), heights)
-        box[slot, edge + xh, rows] = parts[chunk][index].astype(F32)
-
-    all_rows(fill)
+        box[index[0], edge + xh, rows] = bundle[index].astype(F32)
+
+    all_rows(parts, fill)
 
     def moved(ref, xh, steps):
         step_x, step_y, step_z = steps
@@ -278,11 +285,11 @@
     lax.fori_loop(0, capacity // 2, opening, 0)
     lax.fori_loop(capacity // 2, count[0], later, 0)
 
-    def empty(chunk, index, slot, xh, row):
+    def empty(bundle, index, xh, row):
         rows = pl.ds(pl.multiple_of(row, 8), heights)
-        outs[chunk][index] = collected[slot, xh, rows].astype(BF16)
-
-    all_rows(empty)
+        bundle[index] = collected[index[0], xh, rows].astype(BF16)
+
+    all_rows(outs, empty)
 
 
 def spec(count):
@@ -306,15 +313,15 @@
     )(*inputs)
 
 
-def worker_call(extent, place, slots, offsets, count, arrived, constants):
-    capacity = arrived[0].shape[1]
+def worker_call(extent, place, slots, offsets, count, arrived, sent, constants):
+    capacity = arrived[0][-1].shape[-5]
     half, wide = extent // 2, 2 * extent
     padded_x, padded_y = half + SHIFT + 1, extent + 2 * SHIFT
     return call(
-        functools.partial(worker_kernel, extent),
+        functools.partial(worker_kernel, extent, [len(a) for a in arrived], [len(s) for s in sent]),
         4,
-        [place, slots, offsets, count, *arrived, *constants],
-        [jax.ShapeDtypeStruct(a.shape, BF16) for a in arrived],
+        [place, slots, offsets, count, *arrived[0], *arrived[1], *constants],
+        [*sent[0], *sent[1]],
         [
             pltpu.VMEM((capacity, padded_x, padded_y, wide), F32),
             pltpu.VMEM((half, extent, wide), F32),
@@ -331,8 +338,19 @@
     return array if step == 0 else lax.ppermute(array, "pair", [(i, i ^ step) for i in range(total)])
 
 
-def over_grid(array):
-    return lax.all_to_all(array, "grid", 0, 0, tiled=True)
+def over_grid(bundles, total):
+    if len(bundles) == 1:
+        return [lax.all_to_all(bundles[0], "grid", 0, 0, tiled=True)]
+    return [
+        bundle if turn == 0 else lax.ppermute(bundle, "grid", [(i, i ^ turn) for i in range(total)])
+        for turn, bundle in enumerate(bundles)
+    ]
+
+
+def bundle_shapes(split_up, grid_total, single):
+    if split_up:
+        return [jax.ShapeDtypeStruct(single, BF16)] * grid_total
+    return [jax.ShapeDtypeStruct((grid_total, *single), BF16)]
 
 
 def shards(grid_total, pair_total, orbitals, box_list, pair_slots, offsets, pair_count):
@@ -351,18 +369,19 @@
 
     (own,) = call(functools.partial(pieces_kernel, extent), 0, [orbitals], [shape(piece, BF16)], [rows])
     gathered = [over_pair(own, step, pair_total) for step in range(pair_total)]
-    arrived = []
-    for chunk in chunks:
-        bundle = (grid_total, capacity, local, len(chunk), heights, wide)
-        (outgoing,) = call(
-            functools.partial(choose_kernel, pair_total, capacity),
+    arrived, sent = [], []
+    for chunk, split_in, split_out in zip(chunks, SPLIT_IN, SPLIT_OUT):
+        single = (capacity, local, len(chunk), heights, wide)
+        outgoing = call(
+            functools.partial(choose_kernel, pair_total, capacity, len(chunk)),
             2,
             [place, boxes, *(gathered[step] for step in chunk)],
-            [shape(bundle, BF16)],
+            bundle_shapes(split_in, grid_total, single),
             [],
-            flops=CHOOSE_HINT,
+            flops=CHOOSE_HINT[chunk[0] > 0],
         )
-        arrived.append(over_grid(outgoing))
+        arrived.append(over_grid(outgoing, grid_total))
+        sent.append(bundle_shapes(split_out, grid_total, single))
     fields = worker_call(
         extent,
         place,
@@ -370,19 +389,23 @@
         offsets.reshape(-1),
         pair_count.reshape(-1),
         arrived,
+        sent,
         [jnp.asarray(t) for t in tables(extent)],
     )
-    parts = [None] * pair_total
+    fields = (fields[: len(sent[0])], fields[len(sent[0]) :])
+    parts = []
     for chunk, field in reversed(list(zip(chunks, fields))):
+        if parts:
+            field = lax.optimization_barrier((*field, *landed))[: len(field)]
+        landed = over_grid(field, grid_total)
         sums = call(
-            functools.partial(gather_kernel, pair_total, capacity),
+            functools.partial(gather_kernel, pair_total, capacity, len(landed)),
             2,
-            [place, boxes, over_grid(field)],
-            [shape(piece, F32 if step == 0 else BF16) for step in chunk],
+            [place, boxes, *landed],
+            [shape(piece, BF16 if step > 0 else F32) for step in chunk],
             [pltpu.VMEM((orbital_total, local, len(chunk), heights, wide), F32)],
         )
-        for step, value in zip(chunk, sums):
-            parts[step] = over_pair(value, step, pair_total)
+        parts += [over_pair(value, step, pair_total) for step, value in zip(chunk, sums)]
     (result,) = call(
         functools.partial(slab_kernel, extent), 0, parts, [shape(orbitals.shape, F32)], [rows]
     )

time: 120 us -> 114 us (0.950)
  blocking collectives: 17.8 us -> 0 us
  waiting for transfers between devices: 47.7 us -> 56.1 us
  starting transfers between devices: 25.7 us -> 33.5 us
  Pallas kernels: 25.7 us -> 21 us
  local copies, waits for them, and re-layouts: 2.16 us -> 3.37 us
    all_to_all x1 -> x0, blocking collectives: 17.8 us -> none  [over_grid(): return lax.all_to_all(array, 'grid', 0, 0, tiled=True)]
    ppermute x0 -> x14, waiting for transfers between devices: none -> 17.6 us  [over_grid(): lax.ppermute(bundle, 'grid', [(i, i ^ turn) for i in range(total)])]
    ppermute x0 -> x14, starting transfers between devices: none -> 16.3 us  [over_grid(): lax.ppermute(bundle, 'grid', [(i, i ^ turn) for i in range(total)])]
    all_to_all x3 -> x2, waiting for transfers between devices: 21 us -> 10.4 us  [over_grid(): return [lax.all_to_all(bundles[0], 'grid', 0, 0, tiled=True)]]
    ppermute x6, starting transfers between devices: 14.9 us -> 9.9 us  [over_pair(): lax.ppermute(array, 'pair', [(i, i ^ step) for i in range(total)])]
    pallas_call x7, Pallas kernels: 25.7 us -> 21 us  [call(): pl.pallas_call(kernel, out_shape=out_shapes, in_specs=scalars(scalar_coun...]
    all_to_all x3 -> x2, starting transfers between devices: 10.8 us -> 7.28 us  [over_grid(): return [lax.all_to_all(bundles[0], 'grid', 0, 0, tiled=True)]]
    ppermute x6, waiting for transfers between devices: 26.7 us -> 28.1 us  [over_pair(): lax.ppermute(array, 'pair', [(i, i ^ step) for i in range(total)])]
  transfers between devices with their start and end apart: 9 -> 22, of which waited for: 8 -> 11; matrix products, arithmetic and copies ran while one was open for 1% -> 1% of each run, Pallas kernels for 4% -> 4%
where the time goes in v3:
time: 114 us; the launch traced here: 115 us
  waiting for transfers between devices  56.1 us (49%)
  starting transfers between devices  33.5 us (29%)
  Pallas kernels  21 us (18%)
  local copies, waits for them, and re-layouts  3.37 us (3%)
    ppermute x6, waiting for transfers between devices, over_pair(): lax.ppermute(array, 'pair', [(i, i ^ step) for i in range(total)])  28.1 us
    pallas_call x7, Pallas kernels, call(): pl.pallas_call(kernel, out_shape=out_shapes, in_specs=scalars(scalar_coun...  21 us
    ppermute x14, waiting for transfers between devices, over_grid(): lax.ppermute(bundle, 'grid', [(i, i ^ turn) for i in range(total)])  17.6 us
    ppermute x14, starting transfers between devices, over_grid(): lax.ppermute(bundle, 'grid', [(i, i ^ turn) for i in range(total)])  16.3 us
    all_to_all x2, waiting for transfers between devices, over_grid(): return [lax.all_to_all(bundles[0], 'grid', 0, 0, tiled=True)]  10.4 us
    ppermute x6, starting transfers between devices, over_pair(): lax.ppermute(array, 'pair', [(i, i ^ step) for i in range(total)])  9.9 us
    all_to_all x2, starting transfers between devices, over_grid(): return [lax.all_to_all(bundles[0], 'grid', 0, 0, tiled=True)]  7.28 us
    unnamed x21, local copies, waits for them, and re-layouts  3.09 us
  transfers between devices with their start and end apart: 22, of which 11 were waited for; matrix products, arithmetic and copies ran while one was open for 1% of the time, Pallas kernels for 4%

profile of v3, /device:TPU:0, one launch (start us, length us, event | category | flops | bytes accessed | tf_op | source)
XLA Modules:
  0.0 114.9 jit_solution(2662049806935050520)
XLA Ops:
  0.0 0.9 copy-done
  1.0 0.5 shard_map.100.refs_0_
  1.5 0.0 copy-start.6
  1.5 3.1 %collective-permute-start = (bf16[16,4,16,128]{3,2,1,0:T(8,128)(2,1)S(1)}, bf16[16,4,16,128]{3,2,1,0:T(8,128)(2,1)S(1)}, u32[]{:S(2)}, u32[]{:S(2)}) collective-permute-start(bf16[16,4,16,128]{3,2,1,0:T(8,128)(2,1)S(1)} %shard_map.100.refs_0_), channel_id=1, source_target_pairs={{0,1},{1,0},{2,3},{3,2},{4,5},{5,4},{6,7},{7,6},{8,9},{9,8},{10,11... | collective-permute-start | bytes 786440 | tf_op jit(solution)/shard_map/ppermute | solution.py:338
  4.6 2.5 %collective-permute-start.2 = (bf16[16,4,16,128]{3,2,1,0:T(8,128)(2,1)S(1)}, bf16[16,4,16,128]{3,2,1,0:T(8,128)(2,1)S(1)}, u32[]{:S(2)}, u32[]{:S(2)}) collective-permute-start(bf16[16,4,16,128]{3,2,1,0:T(8,128)(2,1)S(1)} %shard_map.100.refs_0_), channel_id=1, source_target_pairs={{0,3},{1,2},{2,1},{3,0},{4,7},{5,6},{6,5},{7,4},{8,11},{9,10},{10,... | collective-permute-start | bytes 786440 | tf_op jit(solution)/shard_map/ppermute | solution.py:338
  7.0 0.1 collective-permute-start.1
  7.2 0.1 copy.14
  7.3 0.1 reshape.12.boxes
  7.4 0.1 pad_add_fusion.place
  7.5 3.8 %collective-permute-done.refs_1_ = bf16[16,4,16,128]{3,2,1,0:T(8,128)(2,1)S(1)} collective-permute-done((bf16[16,4,16,128]{3,2,1,0:T(8,128)(2,1)S(1)}, bf16[16,4,16,128]{3,2,1,0:T(8,128)(2,1)S(1)}, u32[]{:S(2)}, u32[]{:S(2)}) %collective-permute-start) | collective-permute-done | bytes 262176 | tf_op jit(solution)/shard_map/ppermute | solution.py:338
  11.3 1.6 %shard_map.101 = bf16[8,4,4,2,16,128]{5,4,3,2,1,0:T(8,128)(2,1)} custom-call(s32[2]{0:T(128)S(1)} %pad_add_fusion.place, s32[128]{0:T(128)S(1)} %reshape.12.boxes, bf16[16,4,16,128]{3,2,1,0:T(8,128)(2,1)S(1)} %shard_map.100.refs_0_, bf16[16,4,16,128]{3,2,1,0:T(8,128)(2,1)S(1)} %collective-permute-done.refs_1_), custom_call_target="tpu_custom_call" | custom-call | flops 60000002048 | bytes 1573384 | tf_op jit(solution)/shard_map/pallas_call | solution.py:305
  12.9 3.7 %all-to-all-start = ((bf16[8,4,4,2,16,128]{5,4,3,2,1,0:T(8,128)(2,1)}), bf16[8,4,4,2,16,128]{5,4,3,2,1,0:T(8,128)(2,1)S(1)}, u32[]{:S(2)}, u32[]{:S(2)}) async-start(bf16[8,4,4,2,16,128]{5,4,3,2,1,0:T(8,128)(2,1)} %shard_map.101), calls=%async_computation | async-start | bytes 2097152 | tf_op jit(solution)/shard_map/all_to_all | solution.py:343
  16.6 0.0 copy-start.3
  16.6 3.3 %collective-permute-done.2.refs_1_ = bf16[16,4,16,128]{3,2,1,0:T(8,128)(2,1)S(1)} collective-permute-done((bf16[16,4,16,128]{3,2,1,0:T(8,128)(2,1)S(1)}, bf16[16,4,16,128]{3,2,1,0:T(8,128)(2,1)S(1)}, u32[]{:S(2)}, u32[]{:S(2)}) %collective-permute-start.2) | collective-permute-done | bytes 262176 | tf_op jit(solution)/shard_map/ppermute | solution.py:338
  19.9 10.1 %collective-permute-done.1.refs_0_ = bf16[16,4,16,128]{3,2,1,0:T(8,128)(2,1)S(1)} collective-permute-done((bf16[16,4,16,128]{3,2,1,0:T(8,128)(2,1)S(1)}, bf16[16,4,16,128]{3,2,1,0:T(8,128)(2,1)S(1)}, u32[]{:S(2)}, u32[]{:S(2)}) %collective-permute-start.1) | collective-permute-done | bytes 262176 | tf_op jit(solution)/shard_map/ppermute | solution.py:338
  30.0 0.6 shard_map.102
  30.7 0.0 copy-start.4
  30.7 0.1 collective-permute-start.3
  30.8 1.6 %collective-permute-start.4 = (bf16[4,4,2,16,128]{4,3,2,1,0:T(8,128)(2,1)S(1)}, bf16[4,4,2,16,128]{4,3,2,1,0:T(8,128)(2,1)S(1)}, u32[]{:S(2)}, u32[]{:S(2)}) collective-permute-start(bf16[4,4,2,16,128]{4,3,2,1,0:T(8,128)(2,1)S(1)} %get-tuple-element.29), channel_id=1, source_target_pairs={{0,8},{4,12},{8,0},{12,4},{16,24},{20,28},{24,16},{28,20},{1,9},{5... | collective-permute-start | bytes 393224 | tf_op jit(solution)/shard_map/ppermute | solution.py:345
  32.3 0.3 collective-permute-start.5
  32.6 1.5 %collective-permute-start.6 = (bf16[4,4,2,16,128]{4,3,2,1,0:T(8,128)(2,1)S(1)}, bf16[4,4,2,16,128]{4,3,2,1,0:T(8,128)(2,1)S(1)}, u32[]{:S(2)}, u32[]{:S(2)}) collective-permute-start(bf16[4,4,2,16,128]{4,3,2,1,0:T(8,128)(2,1)S(1)} %get-tuple-element.31), channel_id=1, source_target_pairs={{0,16},{4,20},{8,24},{12,28},{16,0},{20,4},{24,8},{28,12},{1,17},{... | collective-permute-start | bytes 393224 | tf_op jit(solution)/shard_map/ppermute | solution.py:345
  34.1 0.2 collective-permute-start.7
  34.3 0.0 collective-permute-done.3.refs_2_
  34.3 2.4 %collective-permute-start.8 = (bf16[4,4,2,16,128]{4,3,2,1,0:T(8,128)(2,1)S(1)}, bf16[4,4,2,16,128]{4,3,2,1,0:T(8,128)(2,1)S(1)}, u32[]{:S(2)}, u32[]{:S(2)}) collective-permute-start(bf16[4,4,2,16,128]{4,3,2,1,0:T(8,128)(2,1)S(1)} %get-tuple-element.33), channel_id=1, source_target_pairs={{0,24},{4,28},{8,16},{12,20},{16,8},{20,12},{24,0},{28,4},{1,25},{... | collective-permute-start | bytes 393224 | tf_op jit(solution)/shard_map/ppermute | solution.py:345
  36.8 0.4 collective-permute-done.4.refs_3_
  37.1 1.3 %collective-permute-start.9 = (bf16[4,4,2,16,128]{4,3,2,1,0:T(8,128)(2,1)S(1)}, bf16[4,4,2,16,128]{4,3,2,1,0:T(8,128)(2,1)S(1)}, u32[]{:S(2)}, u32[]{:S(2)}) collective-permute-start(bf16[4,4,2,16,128]{4,3,2,1,0:T(8,128)(2,1)S(1)} %get-tuple-element.34), channel_id=1, source_target_pairs={{0,28},{4,24},{8,20},{12,16},{16,12},{20,8},{24,4},{28,0},{1,29},{... | collective-permute-start | bytes 393224 | tf_op jit(solution)/shard_map/ppermute | solution.py:345
  39.0 0.1 copy.15
  39.1 0.1 reshape.13.slots
  39.2 0.6 copy-done.7
  39.8 0.1 copy.16
  39.9 0.1 reshape.14.offsets
  40.0 0.0 collective-permute-done.5.refs_4_
  40.0 0.0 collective-permute-done.6.refs_5_
  40.0 6.2 %collective-permute-done.7.refs_6_ = bf16[4,4,2,16,128]{4,3,2,1,0:T(8,128)(2,1)S(1)} collective-permute-done((bf16[4,4,2,16,128]{4,3,2,1,0:T(8,128)(2,1)S(1)}, bf16[4,4,2,16,128]{4,3,2,1,0:T(8,128)(2,1)S(1)}, u32[]{:S(2)}, u32[]{:S(2)}) %collective-permute-start.7) | collective-permute-done | bytes 131104 | tf_op jit(solution)/shard_map/ppermute | solution.py:345
  46.2 0.0 collective-permute-done.8.refs_7_
  46.2 0.0 collective-permute-done.9.refs_8_
  46.2 0.0 all-to-all-done.refs_0_
  46.3 0.0 copy-start.1
  46.3 1.2 %copy-done.1 = f32[64,32,128]{2,1,0:T(8,128)S(1)} copy-done((f32[64,32,128]{2,1,0:T(8,128)S(1)}, f32[64,32,128]{2,1,0:T(8,128)}, u32[]{:S(2)}) %copy-start.1) | copy-done | bytes 1048600
  47.5 15.0 %shard_map.103 = (bf16[8,4,4,2,16,128]{5,4,3,2,1,0:T(8,128)(2,1)}, bf16[4,4,2,16,128]{4,3,2,1,0:T(8,128)(2,1)S(1)}, bf16[4,4,2,16,128]{4,3,2,1,0:T(8,128)(2,1)S(...) custom-call(s32[2]{0:T(128)S(1)} %pad_add_fusion.place, ...), custom_call_target="tpu_custom_call" | custom-call | flops 1811939328 | bytes 5390428 | tf_op jit(solution)/shard_map/pallas_call | solution.py:305
  62.6 4.3 %collective-permute-start.10 = (bf16[4,4,2,16,128]{4,3,2,1,0:T(8,128)(2,1)S(1)}, bf16[4,4,2,16,128]{4,3,2,1,0:T(8,128)(2,1)S(1)}, u32[]{:S(2)}, u32[]{:S(2)}) collective-permute-start(bf16[4,4,2,16,128]{4,3,2,1,0:T(8,128)(2,1)S(1)} %get-tuple-element.36), channel_id=1, source_target_pairs={{0,4},{4,0},{8,12},{12,8},{16,20},{20,16},{24,28},{28,24},{1,5},{5... | collective-permute-start | bytes 393224 | tf_op jit(solution)/shard_map/ppermute | solution.py:345
  66.9 1.4 %collective-permute-start.11 = (bf16[4,4,2,16,128]{4,3,2,1,0:T(8,128)(2,1)S(1)}, bf16[4,4,2,16,128]{4,3,2,1,0:T(8,128)(2,1)S(1)}, u32[]{:S(2)}, u32[]{:S(2)}) collective-permute-start(bf16[4,4,2,16,128]{4,3,2,1,0:T(8,128)(2,1)S(1)} %get-tuple-element.37), channel_id=1, source_target_pairs={{0,8},{4,12},{8,0},{12,4},{16,24},{20,28},{24,16},{28,20},{1,9},{5... | collective-permute-start | bytes 393224 | tf_op jit(solution)/shard_map/ppermute | solution.py:345
  68.3 0.0 collective-permute-start.12
  68.3 1.5 %collective-permute-start.13 = (bf16[4,4,2,16,128]{4,3,2,1,0:T(8,128)(2,1)S(1)}, bf16[4,4,2,16,128]{4,3,2,1,0:T(8,128)(2,1)S(1)}, u32[]{:S(2)}, u32[]{:S(2)}) collective-permute-start(bf16[4,4,2,16,128]{4,3,2,1,0:T(8,128)(2,1)S(1)} %get-tuple-element.39), channel_id=1, source_target_pairs={{0,16},{4,20},{8,24},{12,28},{16,0},{20,4},{24,8},{28,12},{1,17},{... | collective-permute-start | bytes 393224 | tf_op jit(solution)/shard_map/ppermute | solution.py:345
  69.8 0.6 collective-permute-start.14
  70.4 0.0 collective-permute-done.10.refs_1_
  70.4 1.2 %collective-permute-start.15 = (bf16[4,4,2,16,128]{4,3,2,1,0:T(8,128)(2,1)S(1)}, bf16[4,4,2,16,128]{4,3,2,1,0:T(8,128)(2,1)S(1)}, u32[]{:S(2)}, u32[]{:S(2)}) collective-permute-start(bf16[4,4,2,16,128]{4,3,2,1,0:T(8,128)(2,1)S(1)} %get-tuple-element.41), channel_id=1, source_target_pairs={{0,24},{4,28},{8,16},{12,20},{16,8},{20,12},{24,0},{28,4},{1,25},{... | collective-permute-start | bytes 393224 | tf_op jit(solution)/shard_map/ppermute | solution.py:345
  71.6 1.7 %collective-permute-done.11.refs_2_ = bf16[4,4,2,16,128]{4,3,2,1,0:T(8,128)(2,1)S(1)} collective-permute-done((bf16[4,4,2,16,128]{4,3,2,1,0:T(8,128)(2,1)S(1)}, bf16[4,4,2,16,128]{4,3,2,1,0:T(8,128)(2,1)S(1)}, u32[]{:S(2)}, u32[]{:S(2)}) %collective-permute-start.11) | collective-permute-done | bytes 131104 | tf_op jit(solution)/shard_map/ppermute | solution.py:345
  73.2 0.0 collective-permute-start.16
  73.2 1.8 %collective-permute-done.12.refs_3_ = bf16[4,4,2,16,128]{4,3,2,1,0:T(8,128)(2,1)S(1)} collective-permute-done((bf16[4,4,2,16,128]{4,3,2,1,0:T(8,128)(2,1)S(1)}, bf16[4,4,2,16,128]{4,3,2,1,0:T(8,128)(2,1)S(1)}, u32[]{:S(2)}, u32[]{:S(2)}) %collective-permute-start.12) | collective-permute-done | bytes 131104 | tf_op jit(solution)/shard_map/ppermute | solution.py:345
  75.0 0.0 collective-permute-done.13.refs_4_
  75.0 7.6 %collective-permute-done.14.refs_5_ = bf16[4,4,2,16,128]{4,3,2,1,0:T(8,128)(2,1)S(1)} collective-permute-done((bf16[4,4,2,16,128]{4,3,2,1,0:T(8,128)(2,1)S(1)}, bf16[4,4,2,16,128]{4,3,2,1,0:T(8,128)(2,1)S(1)}, u32[]{:S(2)}, u32[]{:S(2)}) %collective-permute-start.14) | collective-permute-done | bytes 131104 | tf_op jit(solution)/shard_map/ppermute | solution.py:345
  82.6 0.0 collective-permute-done.16.refs_7_
  82.6 3.6 %all-to-all-start.1 = ((bf16[8,4,4,2,16,128]{5,4,3,2,1,0:T(8,128)(2,1)}), bf16[8,4,4,2,16,128]{5,4,3,2,1,0:T(8,128)(2,1)S(1)}, u32[]{:S(2)}, u32[]{:S(2)}) async-start(bf16[8,4,4,2,16,128]{5,4,3,2,1,0:T(8,128)(2,1)} %get-tuple-element.46), calls=%async_computation.1 | async-start | bytes 2097152 | tf_op jit(solution)/shard_map/all_to_all | solution.py:343
  86.1 0.9 shard_map.104
  87.1 0.1 collective-permute-start.17
  87.1 3.9 %collective-permute-start.18 = (bf16[16,4,16,128]{3,2,1,0:T(8,128)(2,1)S(1)}, bf16[16,4,16,128]{3,2,1,0:T(8,128)(2,1)S(1)}, u32[]{:S(2)}, u32[]{:S(2)}) collective-permute-start(bf16[16,4,16,128]{3,2,1,0:T(8,128)(2,1)S(1)} %get-tuple-element.44), channel_id=1, source_target_pairs={{0,3},{1,2},{2,1},{3,0},{4,7},{5,6},{6,5},{7,4},{8,11},{9,10},{10,... | collective-permute-start | bytes 786440 | tf_op jit(solution)/shard_map/ppermute | solution.py:338
  91.0 10.4 %all-to-all-done.1.refs_0_ = bf16[8,4,4,2,16,128]{5,4,3,2,1,0:T(8,128)(2,1)S(1)} async-done(((bf16[8,4,4,2,16,128]{5,4,3,2,1,0:T(8,128)(2,1)}), bf16[8,4,4,2,16,128]{5,4,3,2,1,0:T(8,128)(2,1)S(1)}, u32[]{:S(2)}, u32[]{:S(2)}) %all-to-all-start.1) | async-done | bytes 1048608 | tf_op jit(solution)/shard_map/all_to_all | solution.py:343
  101.5 0.9 shard_map.105
  102.4 0.3 collective-permute-start.19
  102.7 5.7 %collective-permute-done.17.refs_0_ = bf16[16,4,16,128]{3,2,1,0:T(8,128)(2,1)S(1)} collective-permute-done((bf16[16,4,16,128]{3,2,1,0:T(8,128)(2,1)S(1)}, bf16[16,4,16,128]{3,2,1,0:T(8,128)(2,1)S(1)}, u32[]{:S(2)}, u32[]{:S(2)}) %collective-permute-start.17) | collective-permute-done | bytes 262176 | tf_op jit(solution)/shard_map/ppermute | solution.py:338
  108.4 0.0 collective-permute-done.18.refs_1_
  108.4 5.1 %collective-permute-done.19.refs_3_ = bf16[16,4,16,128]{3,2,1,0:T(8,128)(2,1)S(1)} collective-permute-done((bf16[16,4,16,128]{3,2,1,0:T(8,128)(2,1)S(1)}, bf16[16,4,16,128]{3,2,1,0:T(8,128)(2,1)S(1)}, u32[]{:S(2)}, u32[]{:S(2)}) %collective-permute-start.19) | collective-permute-done | bytes 262176 | tf_op jit(solution)/shard_map/ppermute | solution.py:338
  113.5 1.3 %shard_map.106 = f32[8,16,1024]{2,1,0:T(8,128)} custom-call(bf16[16,4,16,128]{3,2,1,0:T(8,128)(2,1)S(1)} %collective-permute-done.17.refs_0_, bf16[16,4,16,128]{3,2,1,0:T(8,128)(2,1)S(1)} %collective-permute-done.18.refs_1_, f32[16,4,16,128]{3,2,1,0:T(8,128)S(1)} %get-tuple-element.47.refs_2_, bf16[16,4,16,128]{3,2,1,0:T(8,128)(2,1)S(1)} %collective-permute-done.19.refs_3_), custom_call_target="tpu_custom_call" | custom-call | bytes 1835008 | tf_op jit(solution)/shard_map/pallas_call | solution.py:305
  (12 shorter events, 0.0 us)
Async XLA Ops:
  0.0 0.9 copy-start
  1.5 5.7 %copy-start.6 = (s32[8,4,4]{0,2,1:T(4,128)S(1)}, s32[8,4,4]{0,2,1:T(4,128)}, u32[]{:S(2)}) copy-start(s32[8,4,4]{0,2,1:T(4,128)} %param.11) | copy-start | bytes 1540
  1.5 9.8 %collective-permute-start = (bf16[16,4,16,128]{3,2,1,0:T(8,128)(2,1)S(1)}, bf16[16,4,16,128]{3,2,1,0:T(8,128)(2,1)S(1)}, u32[]{:S(2)}, u32[]{:S(2)}) collective-permute-start(bf16[16,4,16,128]{3,2,1,0:T(8,128)(2,1)S(1)} %shard_map.100.refs_0_), channel_id=1, source_target_pairs={{0,1},{1,0},{2,3},{3,2},{4,5},{5,4},{6,7},{7,6},{8,9},{9,8},{10,11... | collective-permute-start | bytes 786440 | tf_op jit(solution)/shard_map/ppermute | solution.py:338
  4.6 15.4 %collective-permute-start.2 = (bf16[16,4,16,128]{3,2,1,0:T(8,128)(2,1)S(1)}, bf16[16,4,16,128]{3,2,1,0:T(8,128)(2,1)S(1)}, u32[]{:S(2)}, u32[]{:S(2)}) collective-permute-start(bf16[16,4,16,128]{3,2,1,0:T(8,128)(2,1)S(1)} %shard_map.100.refs_0_), channel_id=1, source_target_pairs={{0,3},{1,2},{2,1},{3,0},{4,7},{5,6},{6,5},{7,4},{8,11},{9,10},{10,... | collective-permute-start | bytes 786440 | tf_op jit(solution)/shard_map/ppermute | solution.py:338
  7.0 23.0 %collective-permute-start.1 = (bf16[16,4,16,128]{3,2,1,0:T(8,128)(2,1)S(1)}, bf16[16,4,16,128]{3,2,1,0:T(8,128)(2,1)S(1)}, u32[]{:S(2)}, u32[]{:S(2)}) collective-permute-start(bf16[16,4,16,128]{3,2,1,0:T(8,128)(2,1)S(1)} %shard_map.100.refs_0_), channel_id=1, source_target_pairs={{0,2},{1,3},{2,0},{3,1},{4,6},{5,7},{6,4},{7,5},{8,10},{9,11},{10,... | collective-permute-start | bytes 786440 | tf_op jit(solution)/shard_map/ppermute | solution.py:338
  12.9 33.4 %all-to-all-start = ((bf16[8,4,4,2,16,128]{5,4,3,2,1,0:T(8,128)(2,1)}), bf16[8,4,4,2,16,128]{5,4,3,2,1,0:T(8,128)(2,1)S(1)}, u32[]{:S(2)}, u32[]{:S(2)}) async-start(bf16[8,4,4,2,16,128]{5,4,3,2,1,0:T(8,128)(2,1)} %shard_map.101), calls=%async_computation | async-start | bytes 2097152 | tf_op jit(solution)/shard_map/all_to_all | solution.py:343
  16.6 29.6 %copy-start.2 = (bf16[384,128]{1,0:T(8,128)(2,1)S(1)}, bf16[384,128]{1,0:T(8,128)(2,1)}, u32[]{:S(2)}) copy-start(bf16[384,128]{1,0:T(8,128)(2,1)} %constant.22.clone.refs_12_) | copy-start | bytes 294916
  16.6 29.6 %copy-start.3 = (bf16[64,192]{1,0:T(8,128)(2,1)S(1)}, bf16[64,192]{1,0:T(8,128)(2,1)}, u32[]{:S(2)}) copy-start(bf16[64,192]{1,0:T(8,128)(2,1)} %constant.19.clone.refs_9_) | copy-start | bytes 73732
  30.0 9.0 %copy-start.8 = (s32[1,1,4,2]{2,3,1,0:T(2,128)S(1)}, s32[1,1,4,2]{2,3,1,0:T(2,128)}, u32[]{:S(2)}) copy-start(s32[1,1,4,2]{2,3,1,0:T(2,128)} %param.12) | copy-start | bytes 100
  30.0 16.2 %copy-start.5 = (bf16[64,96]{1,0:T(8,128)(2,1)S(1)}, bf16[64,96]{1,0:T(8,128)(2,1)}, u32[]{:S(2)}) copy-start(bf16[64,96]{1,0:T(8,128)(2,1)} %constant.20.clone.refs_10_) | copy-start | bytes 36868
  30.7 15.6 %copy-start.4 = (bf16[64,96]{1,0:T(8,128)(2,1)S(1)}, bf16[64,96]{1,0:T(8,128)(2,1)}, u32[]{:S(2)}) copy-start(bf16[64,96]{1,0:T(8,128)(2,1)} %constant.21.clone.refs_11_) | copy-start | bytes 36868
  30.7 3.6 %collective-permute-start.3 = (bf16[4,4,2,16,128]{4,3,2,1,0:T(8,128)(2,1)S(1)}, bf16[4,4,2,16,128]{4,3,2,1,0:T(8,128)(2,1)S(1)}, u32[]{:S(2)}, u32[]{:S(2)}) collective-permute-start(bf16[4,4,2,16,128]{4,3,2,1,0:T(8,128)(2,1)S(1)} %get-tuple-element.28), channel_id=1, source_target_pairs={{0,4},{4,0},{8,12},{12,8},{16,20},{20,16},{24,28},{28,24},{1,5},{5... | collective-permute-start | bytes 393224 | tf_op jit(solution)/shard_map/ppermute | solution.py:345
  30.8 6.4 %collective-permute-start.4 = (bf16[4,4,2,16,128]{4,3,2,1,0:T(8,128)(2,1)S(1)}, bf16[4,4,2,16,128]{4,3,2,1,0:T(8,128)(2,1)S(1)}, u32[]{:S(2)}, u32[]{:S(2)}) collective-permute-start(bf16[4,4,2,16,128]{4,3,2,1,0:T(8,128)(2,1)S(1)} %get-tuple-element.29), channel_id=1, source_target_pairs={{0,8},{4,12},{8,0},{12,4},{16,24},{20,28},{24,16},{28,20},{1,9},{5... | collective-permute-start | bytes 393224 | tf_op jit(solution)/shard_map/ppermute | solution.py:345
  32.3 7.7 %collective-permute-start.5 = (bf16[4,4,2,16,128]{4,3,2,1,0:T(8,128)(2,1)S(1)}, bf16[4,4,2,16,128]{4,3,2,1,0:T(8,128)(2,1)S(1)}, u32[]{:S(2)}, u32[]{:S(2)}) collective-permute-start(bf16[4,4,2,16,128]{4,3,2,1,0:T(8,128)(2,1)S(1)} %get-tuple-element.30), channel_id=1, source_target_pairs={{0,12},{4,8},{8,4},{12,0},{16,28},{20,24},{24,20},{28,16},{1,13},{... | collective-permute-start | bytes 393224 | tf_op jit(solution)/shard_map/ppermute | solution.py:345
  32.6 7.4 %collective-permute-start.6 = (bf16[4,4,2,16,128]{4,3,2,1,0:T(8,128)(2,1)S(1)}, bf16[4,4,2,16,128]{4,3,2,1,0:T(8,128)(2,1)S(1)}, u32[]{:S(2)}, u32[]{:S(2)}) collective-permute-start(bf16[4,4,2,16,128]{4,3,2,1,0:T(8,128)(2,1)S(1)} %get-tuple-element.31), channel_id=1, source_target_pairs={{0,16},{4,20},{8,24},{12,28},{16,0},{20,4},{24,8},{28,12},{1,17},{... | collective-permute-start | bytes 393224 | tf_op jit(solution)/shard_map/ppermute | solution.py:345
  34.1 12.1 %collective-permute-start.7 = (bf16[4,4,2,16,128]{4,3,2,1,0:T(8,128)(2,1)S(1)}, bf16[4,4,2,16,128]{4,3,2,1,0:T(8,128)(2,1)S(1)}, u32[]{:S(2)}, u32[]{:S(2)}) collective-permute-start(bf16[4,4,2,16,128]{4,3,2,1,0:T(8,128)(2,1)S(1)} %get-tuple-element.32), channel_id=1, source_target_pairs={{0,20},{4,16},{8,28},{12,24},{16,4},{20,0},{24,12},{28,8},{1,21},{... | collective-permute-start | bytes 393224 | tf_op jit(solution)/shard_map/ppermute | solution.py:345
  34.3 11.9 %collective-permute-start.8 = (bf16[4,4,2,16,128]{4,3,2,1,0:T(8,128)(2,1)S(1)}, bf16[4,4,2,16,128]{4,3,2,1,0:T(8,128)(2,1)S(1)}, u32[]{:S(2)}, u32[]{:S(2)}) collective-permute-start(bf16[4,4,2,16,128]{4,3,2,1,0:T(8,128)(2,1)S(1)} %get-tuple-element.33), channel_id=1, source_target_pairs={{0,24},{4,28},{8,16},{12,20},{16,8},{20,12},{24,0},{28,4},{1,25},{... | collective-permute-start | bytes 393224 | tf_op jit(solution)/shard_map/ppermute | solution.py:345
  37.1 9.1 %collective-permute-start.9 = (bf16[4,4,2,16,128]{4,3,2,1,0:T(8,128)(2,1)S(1)}, bf16[4,4,2,16,128]{4,3,2,1,0:T(8,128)(2,1)S(1)}, u32[]{:S(2)}, u32[]{:S(2)}) collective-permute-start(bf16[4,4,2,16,128]{4,3,2,1,0:T(8,128)(2,1)S(1)} %get-tuple-element.34), channel_id=1, source_target_pairs={{0,28},{4,24},{8,20},{12,16},{16,12},{20,8},{24,4},{28,0},{1,29},{... | collective-permute-start | bytes 393224 | tf_op jit(solution)/shard_map/ppermute | solution.py:345
  39.1 0.7 copy-start.7
  46.3 1.2 %copy-start.1 = (f32[64,32,128]{2,1,0:T(8,128)S(1)}, f32[64,32,128]{2,1,0:T(8,128)}, u32[]{:S(2)}) copy-start(f32[64,32,128]{2,1,0:T(8,128)} %constant.23.clone.refs_13_) | copy-start | bytes 3145732
  62.6 7.8 %collective-permute-start.10 = (bf16[4,4,2,16,128]{4,3,2,1,0:T(8,128)(2,1)S(1)}, bf16[4,4,2,16,128]{4,3,2,1,0:T(8,128)(2,1)S(1)}, u32[]{:S(2)}, u32[]{:S(2)}) collective-permute-start(bf16[4,4,2,16,128]{4,3,2,1,0:T(8,128)(2,1)S(1)} %get-tuple-element.36), channel_id=1, source_target_pairs={{0,4},{4,0},{8,12},{12,8},{16,20},{20,16},{24,28},{28,24},{1,5},{5... | collective-permute-start | bytes 393224 | tf_op jit(solution)/shard_map/ppermute | solution.py:345
  66.9 6.4 %collective-permute-start.11 = (bf16[4,4,2,16,128]{4,3,2,1,0:T(8,128)(2,1)S(1)}, bf16[4,4,2,16,128]{4,3,2,1,0:T(8,128)(2,1)S(1)}, u32[]{:S(2)}, u32[]{:S(2)}) collective-permute-start(bf16[4,4,2,16,128]{4,3,2,1,0:T(8,128)(2,1)S(1)} %get-tuple-element.37), channel_id=1, source_target_pairs={{0,8},{4,12},{8,0},{12,4},{16,24},{20,28},{24,16},{28,20},{1,9},{5... | collective-permute-start | bytes 393224 | tf_op jit(solution)/shard_map/ppermute | solution.py:345
  68.3 6.7 %collective-permute-start.12 = (bf16[4,4,2,16,128]{4,3,2,1,0:T(8,128)(2,1)S(1)}, bf16[4,4,2,16,128]{4,3,2,1,0:T(8,128)(2,1)S(1)}, u32[]{:S(2)}, u32[]{:S(2)}) collective-permute-start(bf16[4,4,2,16,128]{4,3,2,1,0:T(8,128)(2,1)S(1)} %get-tuple-element.38), channel_id=1, source_target_pairs={{0,12},{4,8},{8,4},{12,0},{16,28},{20,24},{24,20},{28,16},{1,13},{... | collective-permute-start | bytes 393224 | tf_op jit(solution)/shard_map/ppermute | solution.py:345
  68.3 6.7 %collective-permute-start.13 = (bf16[4,4,2,16,128]{4,3,2,1,0:T(8,128)(2,1)S(1)}, bf16[4,4,2,16,128]{4,3,2,1,0:T(8,128)(2,1)S(1)}, u32[]{:S(2)}, u32[]{:S(2)}) collective-permute-start(bf16[4,4,2,16,128]{4,3,2,1,0:T(8,128)(2,1)S(1)} %get-tuple-element.39), channel_id=1, source_target_pairs={{0,16},{4,20},{8,24},{12,28},{16,0},{20,4},{24,8},{28,12},{1,17},{... | collective-permute-start | bytes 393224 | tf_op jit(solution)/shard_map/ppermute | solution.py:345
  69.8 12.7 %collective-permute-start.14 = (bf16[4,4,2,16,128]{4,3,2,1,0:T(8,128)(2,1)S(1)}, bf16[4,4,2,16,128]{4,3,2,1,0:T(8,128)(2,1)S(1)}, u32[]{:S(2)}, u32[]{:S(2)}) collective-permute-start(bf16[4,4,2,16,128]{4,3,2,1,0:T(8,128)(2,1)S(1)} %get-tuple-element.40), channel_id=1, source_target_pairs={{0,20},{4,16},{8,28},{12,24},{16,4},{20,0},{24,12},{28,8},{1,21},{... | collective-permute-start | bytes 393224 | tf_op jit(solution)/shard_map/ppermute | solution.py:345
  70.4 12.2 %collective-permute-start.15 = (bf16[4,4,2,16,128]{4,3,2,1,0:T(8,128)(2,1)S(1)}, bf16[4,4,2,16,128]{4,3,2,1,0:T(8,128)(2,1)S(1)}, u32[]{:S(2)}, u32[]{:S(2)}) collective-permute-start(bf16[4,4,2,16,128]{4,3,2,1,0:T(8,128)(2,1)S(1)} %get-tuple-element.41), channel_id=1, source_target_pairs={{0,24},{4,28},{8,16},{12,20},{16,8},{20,12},{24,0},{28,4},{1,25},{... | collective-permute-start | bytes 393224 | tf_op jit(solution)/shard_map/ppermute | solution.py:345
  73.2 9.3 %collective-permute-start.16 = (bf16[4,4,2,16,128]{4,3,2,1,0:T(8,128)(2,1)S(1)}, bf16[4,4,2,16,128]{4,3,2,1,0:T(8,128)(2,1)S(1)}, u32[]{:S(2)}, u32[]{:S(2)}) collective-permute-start(bf16[4,4,2,16,128]{4,3,2,1,0:T(8,128)(2,1)S(1)} %get-tuple-element.42), channel_id=1, source_target_pairs={{0,28},{4,24},{8,20},{12,16},{16,12},{20,8},{24,4},{28,0},{1,29},{... | collective-permute-start | bytes 393224 | tf_op jit(solution)/shard_map/ppermute | solution.py:345
  82.6 18.9 %all-to-all-start.1 = ((bf16[8,4,4,2,16,128]{5,4,3,2,1,0:T(8,128)(2,1)}), bf16[8,4,4,2,16,128]{5,4,3,2,1,0:T(8,128)(2,1)S(1)}, u32[]{:S(2)}, u32[]{:S(2)}) async-start(bf16[8,4,4,2,16,128]{5,4,3,2,1,0:T(8,128)(2,1)} %get-tuple-element.46), calls=%async_computation.1 | async-start | bytes 2097152 | tf_op jit(solution)/shard_map/all_to_all | solution.py:343
  87.1 21.4 %collective-permute-start.17 = (bf16[16,4,16,128]{3,2,1,0:T(8,128)(2,1)S(1)}, bf16[16,4,16,128]{3,2,1,0:T(8,128)(2,1)S(1)}, u32[]{:S(2)}, u32[]{:S(2)}) collective-permute-start(bf16[16,4,16,128]{3,2,1,0:T(8,128)(2,1)S(1)} %get-tuple-element.43), channel_id=1, source_target_pairs={{0,2},{1,3},{2,0},{3,1},{4,6},{5,7},{6,4},{7,5},{8,10},{9,11},{10,... | collective-permute-start | bytes 786440 | tf_op jit(solution)/shard_map/ppermute | solution.py:338
  87.1 21.3 %collective-permute-start.18 = (bf16[16,4,16,128]{3,2,1,0:T(8,128)(2,1)S(1)}, bf16[16,4,16,128]{3,2,1,0:T(8,128)(2,1)S(1)}, u32[]{:S(2)}, u32[]{:S(2)}) collective-permute-start(bf16[16,4,16,128]{3,2,1,0:T(8,128)(2,1)S(1)} %get-tuple-element.44), channel_id=1, source_target_pairs={{0,3},{1,2},{2,1},{3,0},{4,7},{5,6},{6,5},{7,4},{8,11},{9,10},{10,... | collective-permute-start | bytes 786440 | tf_op jit(solution)/shard_map/ppermute | solution.py:338
  102.4 11.1 %collective-permute-start.19 = (bf16[16,4,16,128]{3,2,1,0:T(8,128)(2,1)S(1)}, bf16[16,4,16,128]{3,2,1,0:T(8,128)(2,1)S(1)}, u32[]{:S(2)}, u32[]{:S(2)}) collective-permute-start(bf16[16,4,16,128]{3,2,1,0:T(8,128)(2,1)S(1)} %get-tuple-element.48), channel_id=1, source_target_pairs={{0,1},{1,0},{2,3},{3,2},{4,5},{5,4},{6,7},{7,6},{8,9},{9,8},{10,11... | collective-permute-start | bytes 786440 | tf_op jit(solution)/shard_map/ppermute | solution.py:338
